TPU v7x, 256 devices: a whole 4x4x8 slice. The times are simulated.
256 devices in a mesh: gx: 8 (over y, core), gy: 8 (over z_lo, x), gz: 4 (over z_hi).
Axes of the slice: x: 4, y: 4, z: 8 (z_hi: 4, z_lo: 2; z = z_hi * 2 + z_lo), core: 2. Of those that a mesh axis runs over, the one named last changes fastest.
Arguments:
- distribution_functions: float32 [27, 64, 64, 512], P(None, 'gx', 'gy', 'gz'), as said below
- gaseous_thermal_state: float32 [64, 64, 512], P('gx', 'gy', 'gz'), may hold values from 0.8 to 1.2
- moisture_fraction: float32 [64, 64, 512], P('gx', 'gy', 'gz'), may hold values from 0 to 0.2
- parcel_lowest_node: int32 [3, 8, 8, 4, 2048], P(None, 'gx', 'gy', 'gz'), may hold values from -1 to 127, as said below
- parcel_fractional_shift: float32 [3, 8, 8, 4, 2048], P(None, 'gx', 'gy', 'gz'), may hold values from 0 to 1
- parcel_motion: float32 [3, 8, 8, 4, 2048], P(None, 'gx', 'gy', 'gz'), may hold values from -0.8 to 0.8
- parcel_thermal_state: float32 [8, 8, 4, 2048], P('gx', 'gy', 'gz'), may hold values from 0.3 to 0.7
- parcel_relaxation_factor: float32 [8, 8, 4, 2048], P('gx', 'gy', 'gz'), may hold values from 0.05 to 0.5
- parcel_live_number: int32 [8, 8, 4], P('gx', 'gy', 'gz'), may hold values from 128 to 2048, as said below
Outputs:
- distribution_functions_next: float32 [27, 64, 64, 512], P(None, 'gx', 'gy', 'gz')
- temperature_out: float32 [64, 64, 512], P('gx', 'gy', 'gz')
- vapour_out: float32 [64, 64, 512], P('gx', 'gy', 'gz')
- parcel_motion_after_drag: float32 [3, 8, 8, 4, 2048], P(None, 'gx', 'gy', 'gz')
Inputs may be any that keep to these rules, and one draw needn't show every extreme that they name: `parcel_lowest_node`: row 0 lies in -1 to 7, row 1 in -1 to 7, row 2 in -1 to 127. `parcel_live_number`: every count is a multiple of 128 and at least 128; some block holds exactly 2048 live droplets. `distribution_functions`: every population is positive.
All inputs are finite; a program needn't handle non-finite values.
Results may differ from a plain program's by a relative error of at most 0.000078.
Values sent between devices are 32-bit elements; how exact they have to be, the bound alone decides.
A program may use at most 64 MiB of HBM per device.

v0:
```python
import jax
import jax.numpy as jnp
from jax import lax
from jax.sharding import PartitionSpec as P

TILE = 128


relax_time = 0.8
load_ratio = 2.0
thermal_exchange_factor = 1.0
equilibrium_vapor_factor = 0.05


def with_halo(block, sides, width):
    for axis, dim in sides:
        count = lax.axis_size(axis)
        forward = [(i, i + 1) for i in range(count - 1)]
        forward.append((count - 1, 0))
        backward = [(target, source) for source, target in forward]
        low = lax.ppermute(
            lax.slice_in_dim(block, block.shape[dim] - width, None, axis=dim), axis, forward
        )
        high = lax.ppermute(lax.slice_in_dim(block, 0, width, axis=dim), axis, backward)
        block = jnp.concatenate([low, block, high], axis=dim)
    return block


def lattice_table():
    return [(label // 9 - 1, label // 3 % 3 - 1, label % 3 - 1) for label in range(27)]


def lattice_weight(label):
    value = 1.0
    for step in lattice_table()[label]:
        value = value * (2.0 / 3.0 if step == 0 else 1.0 / 6.0)
    return value


def moments(distribution_functions):
    table = lattice_table()
    density = distribution_functions[0]
    for label in range(1, 27):
        density = density + distribution_functions[label]
    gaseous_motion = []
    for axis_num in range(3):
        total = jnp.zeros_like(density)
        for label in range(27):
            if table[label][axis_num] == 1:
                total = total + distribution_functions[label]
            elif table[label][axis_num] == -1:
                total = total - distribution_functions[label]
        gaseous_motion.append(total / density)
    return (density, gaseous_motion)


def relax_one(population, label, density, gaseous_motion, speed, feedback_terms_mesh):
    step_x, step_y, step_z = lattice_table()[label]
    weight = lattice_weight(label)
    along = (
        float(step_x) * gaseous_motion[0]
        + float(step_y) * gaseous_motion[1]
        + float(step_z) * gaseous_motion[2]
    )
    equil = weight * density * (1.0 + 3.0 * along + 4.5 * along * along - 1.5 * speed)
    push = (
        float(step_x) * feedback_terms_mesh[0]
        + float(step_y) * feedback_terms_mesh[1]
        + float(step_z) * feedback_terms_mesh[2]
    )
    return (
        population
        - (population - equil) / relax_time
        + weight * (feedback_terms_mesh[4] + 3.0 * push)
    )


def parcel_exchange_parts(
    interpolated, parcel_motion, parcel_thermal_state, parcel_relaxation_factor
):
    increment = parcel_relaxation_factor[None] * (interpolated[0:3] - parcel_motion)
    thermal_exchange = (
        thermal_exchange_factor
        * parcel_relaxation_factor
        * (parcel_thermal_state - interpolated[3])
    )
    equilibrium_vapor = equilibrium_vapor_factor * jnp.exp(3.0 * (parcel_thermal_state - 0.5))
    mass = parcel_relaxation_factor * (equilibrium_vapor - interpolated[4])
    exchange_parts = jnp.concatenate(
        [-load_ratio * increment, thermal_exchange[None], mass[None]], axis=0
    )
    return (increment, exchange_parts)


def axis_weights(base_row, frac_row, length):
    cells = lax.broadcasted_iota(jnp.int32, (length, base_row.shape[0]), 0)
    lower = jnp.where(cells == base_row[None] + 1, 1.0 - frac_row[None], 0.0)
    upper = jnp.where(cells == base_row[None] + 2, frac_row[None], 0.0)
    return lower + upper


def fold_rim(array, axis_num, count):
    inner = lax.slice_in_dim(array, 2, count + 2, axis=axis_num)
    lower = lax.slice_in_dim(array, 0, 1, axis=axis_num)
    upper = lax.slice_in_dim(array, count + 3, count + 4, axis=axis_num)
    widths_low = [(0, 0)] * array.ndim
    widths_low[axis_num] = (0, count - 1)
    widths_high = [(0, 0)] * array.ndim
    widths_high[axis_num] = (count - 1, 0)
    return inner + jnp.pad(lower, widths_low) + jnp.pad(upper, widths_high)


def on_device(
    distribution_functions,
    gaseous_thermal_state,
    moisture_fraction,
    parcel_lowest_node,
    parcel_fractional_shift,
    parcel_motion,
    parcel_thermal_state,
    parcel_relaxation_factor,
    parcel_live_number,
):
    patch_nodes_first, patch_nodes_second, patch_nodes_third = gaseous_thermal_state.shape
    ext_x = patch_nodes_first + 2
    ext_y = patch_nodes_second + 2
    ext_z = patch_nodes_third + 2
    density, gaseous_motion = moments(distribution_functions)
    moment_quantities = jnp.stack(gaseous_motion + [gaseous_thermal_state, moisture_fraction])
    rimmed = with_halo(moment_quantities, (("gx", 1), ("gy", 2), ("gz", 3)), 1)
    parcel_limit_value = parcel_motion.shape[-1]
    base_all = parcel_lowest_node.reshape(3, parcel_limit_value)
    frac_all = parcel_fractional_shift.reshape(3, parcel_limit_value)
    vel_all = parcel_motion.reshape(3, parcel_limit_value)
    thermal_state_every = parcel_thermal_state.reshape(parcel_limit_value)
    rate_all = parcel_relaxation_factor.reshape(parcel_limit_value)
    tile_count = parcel_live_number.reshape(()) // TILE
    deposit_start = jnp.zeros((5, ext_x, ext_y, ext_z), jnp.float32)

    def tile_step(number, carry):
        deposit, moved = carry
        first = number * TILE
        piece_base = lax.dynamic_slice_in_dim(base_all, first, TILE, 1)
        piece_frac = lax.dynamic_slice_in_dim(frac_all, first, TILE, 1)
        piece_vel = lax.dynamic_slice_in_dim(vel_all, first, TILE, 1)
        piece_temp = lax.dynamic_slice_in_dim(thermal_state_every, first, TILE, 0)
        piece_rate = lax.dynamic_slice_in_dim(rate_all, first, TILE, 0)
        weight_x = axis_weights(piece_base[0], piece_frac[0], ext_x)
        weight_y = axis_weights(piece_base[1], piece_frac[1], ext_y)
        weight_z = axis_weights(piece_base[2], piece_frac[2], ext_z)
        plane = weight_x[:, None, :] * weight_y[None, :, :]
        along_z = jnp.einsum(
            "cxyz,zp->cxyp",
            rimmed,
            weight_z,
            precision=lax.Precision.HIGHEST,
            preferred_element_type=jnp.float32,
        )
        interpolated = jnp.sum(along_z * plane[None], axis=(1, 2))
        increment, exchange_parts = parcel_exchange_parts(
            interpolated, piece_vel, piece_temp, piece_rate
        )
        spread_load = exchange_parts[:, None, None, :] * plane[None]
        deposit = deposit + jnp.einsum(
            "cxyp,zp->cxyz",
            spread_load,
            weight_z,
            precision=lax.Precision.HIGHEST,
            preferred_element_type=jnp.float32,
        )
        moved = lax.dynamic_update_slice_in_dim(moved, piece_vel + increment, first, 1)
        return (deposit, moved)

    deposit, moved = lax.fori_loop(0, tile_count, tile_step, (deposit_start, vel_all))
    shared = with_halo(deposit, (("gx", 1), ("gy", 2), ("gz", 3)), 1)
    feedback_terms_mesh = fold_rim(
        fold_rim(fold_rim(shared, 1, patch_nodes_first), 2, patch_nodes_second),
        3,
        patch_nodes_third,
    )
    speed = (
        gaseous_motion[0] * gaseous_motion[0]
        + gaseous_motion[1] * gaseous_motion[1]
        + gaseous_motion[2] * gaseous_motion[2]
    )
    relaxed_all = jnp.stack(
        [
            relax_one(
                distribution_functions[label],
                label,
                density,
                gaseous_motion,
                speed,
                feedback_terms_mesh,
            )
            for label in range(27)
        ]
    )
    table = lattice_table()
    wide = with_halo(relaxed_all, (("gx", 1), ("gy", 2), ("gz", 3)), 1)
    pieces = []
    for label in range(27):
        step_x, step_y, step_z = table[label]
        pieces.append(
            wide[
                label,
                1 - step_x : 1 - step_x + patch_nodes_first,
                1 - step_y : 1 - step_y + patch_nodes_second,
                1 - step_z : 1 - step_z + patch_nodes_third,
            ]
        )
    distribution_functions_next = jnp.stack(pieces)
    return (
        distribution_functions_next,
        gaseous_thermal_state + feedback_terms_mesh[3],
        moisture_fraction + feedback_terms_mesh[4],
        moved.reshape(parcel_motion.shape),
    )


def solution(mesh):
    placed = (
        P(None, "gx", "gy", "gz"),
        P("gx", "gy", "gz"),
        P("gx", "gy", "gz"),
        P(None, "gx", "gy", "gz", None),
        P(None, "gx", "gy", "gz", None),
        P(None, "gx", "gy", "gz", None),
        P("gx", "gy", "gz", None),
        P("gx", "gy", "gz", None),
        P("gx", "gy", "gz"),
    )
    return jax.shard_map(
        on_device,
        mesh=mesh,
        in_specs=placed,
        out_specs=(
            P(None, "gx", "gy", "gz"),
            P("gx", "gy", "gz"),
            P("gx", "gy", "gz"),
            P(None, "gx", "gy", "gz", None),
        ),
        check_vma=False,
    )
```

profile of v0, /device:TPU:24, one launch (start us, length us, event | category | flops | bytes accessed | tf_op | source)
XLA Modules:
  0.0 168.8 jit_solution(15244260971061624920)
XLA Ops:
  0.7 1.2 constant_dynamic-update-slice_fusion.4
  1.9 1.1 constant_dynamic-update-slice_fusion.3
  3.0 1.1 constant_dynamic-update-slice_fusion.2
  4.1 1.7 %collective-permute-start.1 = (f32[5,1,8,128]{3,2,1,0:T(8,128)S(1)}, f32[5,1,8,128]{3,2,1,0:T(8,128)S(1)}, u32[]{:S(2)}, u32[]{:S(2)}) collective-permute-start(f32[5,1,8,128]{3,2,1,0:T(8,128)S(1)} %get-tuple-element.218), channel_id=1, source_target_pairs={{32,0},{64,32},{96,64},{128,96},{160,128},{192,160},{224,192},{0,2... | collective-permute-start | bytes 61448 | tf_op jit(solution)/shard_map/ppermute | solution.py:24
  5.9 1.5 collective-permute-done
  7.4 1.6 collective-permute-start.2
  8.9 2.7 %collective-permute-start.3 = (f32[5,10,1,128]{3,2,1,0:T(1,128)S(1)}, f32[5,10,1,128]{3,2,1,0:T(1,128)S(1)}, u32[]{:S(2)}, u32[]{:S(2)}) collective-permute-start(f32[5,10,1,128]{3,2,1,0:T(1,128)S(1)} %get-tuple-element.214), channel_id=1, source_target_pairs={{4,0},{8,4},{12,8},{16,12},{20,16},{24,20},{28,24},{0,28},{5,1},{9... | collective-permute-start | bytes 76808 | tf_op jit(solution)/shard_map/ppermute | solution.py:24
  11.7 1.7 %collective-permute-done.2 = f32[5,10,1,128]{3,2,1,0:T(1,128)S(1)} collective-permute-done((f32[5,10,1,128]{3,2,1,0:T(1,128)S(1)}, f32[5,10,1,128]{3,2,1,0:T(1,128)S(1)}, u32[]{:S(2)}, u32[]{:S(2)}) %collective-permute-start.2) | collective-permute-done | bytes 25632 | tf_op jit(solution)/shard_map/ppermute | solution.py:21
  13.7 3.3 %collective-permute-start.4 = (f32[5,10,10,1]{3,2,1,0:T(8,128)S(1)}, f32[5,10,10,1]{3,2,1,0:T(8,128)S(1)}, u32[]{:S(2)}, u32[]{:S(2)}) collective-permute-start(f32[5,10,10,1]{3,2,1,0:T(8,128)S(1)} %get-tuple-element.211), channel_id=1, source_target_pairs={{0,1},{1,2},{2,3},{3,0},{4,5},{5,6},{6,7},{7,4},{8,9},{9,10},{10,1... | collective-permute-start | bytes 6008 | tf_op jit(solution)/shard_map/ppermute | solution.py:21
  17.0 3.1 %collective-permute-start.5 = (f32[5,10,10,1]{3,2,1,0:T(8,128)S(1)}, f32[5,10,10,1]{3,2,1,0:T(8,128)S(1)}, u32[]{:S(2)}, u32[]{:S(2)}) collective-permute-start(f32[5,10,10,1]{3,2,1,0:T(8,128)S(1)} %get-tuple-element.212), channel_id=1, source_target_pairs={{1,0},{2,1},{3,2},{0,3},{5,4},{6,5},{7,6},{4,7},{9,8},{10,9},{11,1... | collective-permute-start | bytes 6008 | tf_op jit(solution)/shard_map/ppermute | solution.py:24
  20.9 12.6 %collective-permute-done.4 = f32[5,10,10,1]{3,2,1,0:T(8,128)S(1)} collective-permute-done((f32[5,10,10,1]{3,2,1,0:T(8,128)S(1)}, f32[5,10,10,1]{3,2,1,0:T(8,128)S(1)}, u32[]{:S(2)}, u32[]{:S(2)}) %collective-permute-start.4) | collective-permute-done | bytes 2032 | tf_op jit(solution)/shard_map/ppermute | solution.py:21
  33.5 6.5 %collective-permute-done.5 = f32[5,10,10,1]{3,2,1,0:T(8,128)S(1)} collective-permute-done((f32[5,10,10,1]{3,2,1,0:T(8,128)S(1)}, f32[5,10,10,1]{3,2,1,0:T(8,128)S(1)}, u32[]{:S(2)}, u32[]{:S(2)}) %collective-permute-start.5) | collective-permute-done | bytes 2032 | tf_op jit(solution)/shard_map/ppermute | solution.py:24
  40.7 45.7 %while.14 = (s32[]{:T(128)}, f32[5,10,10,130]{3,2,1,0:T(8,128)S(1)}, f32[3,2048]{1,0:T(4,128)S(1)}, s32[]{:T(128)}, f32[2048]{0:T(1024)}, /*index=5*/s32[3,2048]...) while((s32[]{:T(128)}, ...), condition=%wide.region_2.3_spmd, body=%wide.region_0.2_spmd.sunk | while | flops 200133232 | bytes 1000355 | solution.py:174
  42.5 1.1 convolution_add_fusion.2
  45.3 1.1 convolution_add_fusion.2
  48.2 1.1 convolution_add_fusion.2
  51.1 1.1 convolution_add_fusion.2
  53.9 1.1 convolution_add_fusion.2
  56.8 1.1 convolution_add_fusion.2
  59.6 1.1 convolution_add_fusion.2
  62.5 1.1 convolution_add_fusion.2
  65.4 1.1 convolution_add_fusion.2
  68.2 1.1 convolution_add_fusion.2
  71.1 1.1 convolution_add_fusion.2
  73.9 1.1 convolution_add_fusion.2
  76.8 1.1 convolution_add_fusion.2
  79.7 1.1 convolution_add_fusion.2
  82.5 1.1 convolution_add_fusion.2
  85.4 1.1 convolution_add_fusion.2
  86.5 1.7 %collective-permute-start.7 = (f32[5,1,10,130]{3,2,1,0:T(8,128)S(1)}, f32[5,1,10,130]{3,2,1,0:T(8,128)S(1)}, u32[]{:S(2)}, u32[]{:S(2)}) collective-permute-start(f32[5,1,10,130]{3,2,1,0:T(8,128)S(1)} %get-tuple-element.209), channel_id=1, source_target_pairs={{32,0},{64,32},{96,64},{128,96},{160,128},{192,160},{224,192},{0,2... | collective-permute-start | bytes 78008 | tf_op jit(solution)/shard_map/ppermute | solution.py:24
  88.3 2.1 %collective-permute-done.6 = f32[5,1,10,130]{3,2,1,0:T(8,128)S(1)} collective-permute-done((f32[5,1,10,130]{3,2,1,0:T(8,128)S(1)}, f32[5,1,10,130]{3,2,1,0:T(8,128)S(1)}, u32[]{:S(2)}, u32[]{:S(2)}) %collective-permute-start.6) | collective-permute-done | bytes 26032 | tf_op jit(solution)/shard_map/ppermute | solution.py:21
  90.7 4.1 %collective-permute-start.9 = (f32[5,12,1,130]{3,2,1,0:T(1,128)S(1)}, f32[5,12,1,130]{3,2,1,0:T(1,128)S(1)}, u32[]{:S(2)}, u32[]{:S(2)}) collective-permute-start(f32[5,12,1,130]{3,2,1,0:T(1,128)S(1)} %get-tuple-element.206), channel_id=1, source_target_pairs={{4,0},{8,4},{12,8},{16,12},{20,16},{24,20},{28,24},{0,28},{5,1},{9... | collective-permute-start | bytes 93608 | tf_op jit(solution)/shard_map/ppermute | solution.py:24
  94.8 2.3 %collective-permute-done.8 = f32[5,12,1,130]{3,2,1,0:T(1,128)S(1)} collective-permute-done((f32[5,12,1,130]{3,2,1,0:T(1,128)S(1)}, f32[5,12,1,130]{3,2,1,0:T(1,128)S(1)}, u32[]{:S(2)}, u32[]{:S(2)}) %collective-permute-start.8) | collective-permute-done | bytes 31232 | tf_op jit(solution)/shard_map/ppermute | solution.py:21
  97.0 9.3 %collective-permute-done.9 = f32[5,12,1,130]{3,2,1,0:T(1,128)S(1)} collective-permute-done((f32[5,12,1,130]{3,2,1,0:T(1,128)S(1)}, f32[5,12,1,130]{3,2,1,0:T(1,128)S(1)}, u32[]{:S(2)}, u32[]{:S(2)}) %collective-permute-start.9) | collective-permute-done | bytes 31232 | tf_op jit(solution)/shard_map/ppermute | solution.py:24
  106.9 4.1 %collective-permute-start.11 = (f32[5,12,12,1]{3,2,1,0:T(8,128)S(1)}, f32[5,12,12,1]{3,2,1,0:T(8,128)S(1)}, u32[]{:S(2)}, u32[]{:S(2)}) collective-permute-start(f32[5,12,12,1]{3,2,1,0:T(8,128)S(1)} %get-tuple-element.204), channel_id=1, source_target_pairs={{1,0},{2,1},{3,2},{0,3},{5,4},{6,5},{7,6},{4,7},{9,8},{10,9},{11,1... | collective-permute-start | bytes 8648 | tf_op jit(solution)/shard_map/ppermute | solution.py:24
  111.0 11.3 %collective-permute-done.10 = f32[5,12,12,1]{3,2,1,0:T(8,128)S(1)} collective-permute-done((f32[5,12,12,1]{3,2,1,0:T(8,128)S(1)}, f32[5,12,12,1]{3,2,1,0:T(8,128)S(1)}, u32[]{:S(2)}, u32[]{:S(2)}) %collective-permute-start.10) | collective-permute-done | bytes 2912 | tf_op jit(solution)/shard_map/ppermute | solution.py:21
  125.4 1.7 %collective-permute-start.13 = (f32[27,1,8,128]{3,2,1,0:T(8,128)S(1)}, f32[27,1,8,128]{3,2,1,0:T(8,128)S(1)}, u32[]{:S(2)}, u32[]{:S(2)}) collective-permute-start(f32[27,1,8,128]{3,2,1,0:T(8,128)S(1)} %get-tuple-element.208), channel_id=1, source_target_pairs={{32,0},{64,32},{96,64},{128,96},{160,128},{192,160},{224,192},{0,2... | collective-permute-start | bytes 331784 | tf_op jit(solution)/shard_map/ppermute | solution.py:24
  127.1 2.4 %collective-permute-done.12 = f32[27,1,8,128]{3,2,1,0:T(8,128)S(1)} collective-permute-done((f32[27,1,8,128]{3,2,1,0:T(8,128)S(1)}, f32[27,1,8,128]{3,2,1,0:T(8,128)S(1)}, u32[]{:S(2)}, u32[]{:S(2)}) %collective-permute-start.12) | collective-permute-done | bytes 110624 | tf_op jit(solution)/shard_map/ppermute | solution.py:21
  129.8 5.4 %collective-permute-start.15 = (f32[27,10,1,128]{3,2,1,0:T(1,128)S(1)}, f32[27,10,1,128]{3,2,1,0:T(1,128)S(1)}, u32[]{:S(2)}, u32[]{:S(2)}) collective-permute-start(f32[27,10,1,128]{3,2,1,0:T(1,128)S(1)} %get-tuple-element.202), channel_id=1, source_target_pairs={{4,0},{8,4},{12,8},{16,12},{20,16},{24,20},{28,24},{0,28},{5,1},{9... | collective-permute-start | bytes 414728 | tf_op jit(solution)/shard_map/ppermute | solution.py:24
  135.9 2.6 %collective-permute-done.14 = f32[27,10,1,128]{3,2,1,0:T(1,128)S(1)} collective-permute-done((f32[27,10,1,128]{3,2,1,0:T(1,128)S(1)}, f32[27,10,1,128]{3,2,1,0:T(1,128)S(1)}, u32[]{:S(2)}, u32[]{:S(2)}) %collective-permute-start.14) | collective-permute-done | bytes 138272 | tf_op jit(solution)/shard_map/ppermute | solution.py:21
  138.9 2.9 %fusion.225 = (f32[27,10,10,1]{3,2,1,0:T(8,128)}, f32[27,10,10,1]{3,2,1,0:T(8,128)}) fusion(f32[27,10,10,128]{3,2,1,0:T(8,128)S(1)} %pad_maximum_fusion.1), kind=kLoop, calls=%fused_computation.409 | loop fusion | bytes 43200 | tf_op jit(solution)/shard_map/slice | solution.py:22
  141.8 2.5 %copy.238 = f32[27,10,10,1]{0,3,2,1:T(1,128)S(1)} copy(f32[27,10,10,1]{3,2,1,0:T(8,128)} %get-tuple-element.199) | data formatting | bytes 21600 | tf_op jit(solution)/shard_map/slice | solution.py:22
  144.3 2.5 %copy.236 = f32[27,10,10,1]{0,3,2,1:T(1,128)S(1)} copy(f32[27,10,10,1]{3,2,1,0:T(8,128)} %get-tuple-element.200) | data formatting | bytes 21600 | tf_op jit(solution)/shard_map/slice | solution.py:24
  146.8 3.8 %collective-permute-start.16 = (f32[27,10,10,1]{0,3,2,1:T(1,128)S(1)}, f32[27,10,10,1]{0,3,2,1:T(1,128)}, u32[]{:S(2)}, u32[]{:S(2)}) collective-permute-start(f32[27,10,10,1]{0,3,2,1:T(1,128)S(1)} %copy.236), channel_id=1, source_target_pairs={{1,0},{2,1},{3,2},{0,3},{5,4},{6,5},{7,6},{4,7},{9,8},{10,9},{11,1... | collective-permute-start | bytes 32408 | tf_op jit(solution)/shard_map/ppermute | solution.py:24
  151.2 5.7 %collective-permute-done.17 = f32[27,10,10,1]{0,3,2,1:T(1,128)} collective-permute-done((f32[27,10,10,1]{0,3,2,1:T(1,128)S(1)}, f32[27,10,10,1]{0,3,2,1:T(1,128)}, u32[]{:S(2)}, u32[]{:S(2)}) %collective-permute-start.17) | collective-permute-done | bytes 10832 | tf_op jit(solution)/shard_map/ppermute | solution.py:21
  156.9 2.7 %copy.239 = f32[27,10,10,1]{3,2,1,0:T(8,128)S(1)} copy(f32[27,10,10,1]{0,3,2,1:T(1,128)} %collective-permute-done.17) | data formatting | bytes 21600 | tf_op jit(solution)/shard_map/ppermute | solution.py:21
  159.6 3.9 %copy.237 = f32[27,10,10,1]{3,2,1,0:T(8,128)} copy(f32[27,10,10,1]{0,3,2,1:T(1,128)} %collective-permute-done.16) | data formatting | bytes 21600 | tf_op jit(solution)/shard_map/ppermute | solution.py:24
  164.7 1.5 copy-done
  (280 shorter events, 37.2 us)
Async XLA Ops:
  0.6 3.4 %copy-start.4 = (f32[8,8,128]{2,1,0:T(8,128)S(1)}, f32[8,8,128]{2,1,0:T(8,128)}, u32[]{:S(2)}) copy-start(f32[8,8,128]{2,1,0:T(8,128)} %param.12) | copy-start | bytes 98308
  0.6 3.4 %copy-start.5 = (f32[8,8,128]{2,1,0:T(8,128)S(1)}, f32[8,8,128]{2,1,0:T(8,128)}, u32[]{:S(2)}) copy-start(f32[8,8,128]{2,1,0:T(8,128)} %param.13) | copy-start | bytes 98308
  1.9 18.3 %copy-start.6 = (f32[3,1,1,1,2048]{4,3,2,1,0:T(1,128)S(1)}, f32[3,1,1,1,2048]{4,3,2,1,0:T(1,128)}, u32[]{:S(2)}) copy-start(f32[3,1,1,1,2048]{4,3,2,1,0:T(1,128)} %param.15) | copy-start | bytes 73732
  1.9 18.3 %copy-start.7 = (f32[3,1,1,1,2048]{4,3,2,1,0:T(1,128)S(1)}, f32[3,1,1,1,2048]{4,3,2,1,0:T(1,128)}, u32[]{:S(2)}) copy-start(f32[3,1,1,1,2048]{4,3,2,1,0:T(1,128)} %param.16) | copy-start | bytes 73732
  1.9 19.0 %copy-start.8 = (s32[3,1,1,1,2048]{4,3,2,1,0:T(1,128)S(1)}, s32[3,1,1,1,2048]{4,3,2,1,0:T(1,128)}, u32[]{:S(2)}) copy-start(s32[3,1,1,1,2048]{4,3,2,1,0:T(1,128)} %param.14) | copy-start | bytes 73732
  4.1 3.2 %collective-permute-start = (f32[5,1,8,128]{3,2,1,0:T(8,128)S(1)}, f32[5,1,8,128]{3,2,1,0:T(8,128)S(1)}, u32[]{:S(2)}, u32[]{:S(2)}) collective-permute-start(f32[5,1,8,128]{3,2,1,0:T(8,128)S(1)} %get-tuple-element.217), channel_id=1, source_target_pairs={{0,32},{32,64},{64,96},{96,128},{128,160},{160,192},{192,224},{224... | collective-permute-start | bytes 61448 | tf_op jit(solution)/shard_map/ppermute | solution.py:21
  4.1 3.2 %collective-permute-start.1 = (f32[5,1,8,128]{3,2,1,0:T(8,128)S(1)}, f32[5,1,8,128]{3,2,1,0:T(8,128)S(1)}, u32[]{:S(2)}, u32[]{:S(2)}) collective-permute-start(f32[5,1,8,128]{3,2,1,0:T(8,128)S(1)} %get-tuple-element.218), channel_id=1, source_target_pairs={{32,0},{64,32},{96,64},{128,96},{160,128},{192,160},{224,192},{0,2... | collective-permute-start | bytes 61448 | tf_op jit(solution)/shard_map/ppermute | solution.py:24
  7.4 6.0 %collective-permute-start.2 = (f32[5,10,1,128]{3,2,1,0:T(1,128)S(1)}, f32[5,10,1,128]{3,2,1,0:T(1,128)S(1)}, u32[]{:S(2)}, u32[]{:S(2)}) collective-permute-start(f32[5,10,1,128]{3,2,1,0:T(1,128)S(1)} %get-tuple-element.213), channel_id=1, source_target_pairs={{0,4},{4,8},{8,12},{12,16},{16,20},{20,24},{24,28},{28,0},{1,5},{5... | collective-permute-start | bytes 76808 | tf_op jit(solution)/shard_map/ppermute | solution.py:21
  8.9 4.5 %collective-permute-start.3 = (f32[5,10,1,128]{3,2,1,0:T(1,128)S(1)}, f32[5,10,1,128]{3,2,1,0:T(1,128)S(1)}, u32[]{:S(2)}, u32[]{:S(2)}) collective-permute-start(f32[5,10,1,128]{3,2,1,0:T(1,128)S(1)} %get-tuple-element.214), channel_id=1, source_target_pairs={{4,0},{8,4},{12,8},{16,12},{20,16},{24,20},{28,24},{0,28},{5,1},{9... | collective-permute-start | bytes 76808 | tf_op jit(solution)/shard_map/ppermute | solution.py:24
  13.7 19.8 %collective-permute-start.4 = (f32[5,10,10,1]{3,2,1,0:T(8,128)S(1)}, f32[5,10,10,1]{3,2,1,0:T(8,128)S(1)}, u32[]{:S(2)}, u32[]{:S(2)}) collective-permute-start(f32[5,10,10,1]{3,2,1,0:T(8,128)S(1)} %get-tuple-element.211), channel_id=1, source_target_pairs={{0,1},{1,2},{2,3},{3,0},{4,5},{5,6},{6,7},{7,4},{8,9},{9,10},{10,1... | collective-permute-start | bytes 6008 | tf_op jit(solution)/shard_map/ppermute | solution.py:21
  17.0 23.0 %collective-permute-start.5 = (f32[5,10,10,1]{3,2,1,0:T(8,128)S(1)}, f32[5,10,10,1]{3,2,1,0:T(8,128)S(1)}, u32[]{:S(2)}, u32[]{:S(2)}) collective-permute-start(f32[5,10,10,1]{3,2,1,0:T(8,128)S(1)} %get-tuple-element.212), channel_id=1, source_target_pairs={{1,0},{2,1},{3,2},{0,3},{5,4},{6,5},{7,6},{4,7},{9,8},{10,9},{11,1... | collective-permute-start | bytes 6008 | tf_op jit(solution)/shard_map/ppermute | solution.py:24
  86.5 3.9 %collective-permute-start.6 = (f32[5,1,10,130]{3,2,1,0:T(8,128)S(1)}, f32[5,1,10,130]{3,2,1,0:T(8,128)S(1)}, u32[]{:S(2)}, u32[]{:S(2)}) collective-permute-start(f32[5,1,10,130]{3,2,1,0:T(8,128)S(1)} %get-tuple-element.210), channel_id=1, source_target_pairs={{0,32},{32,64},{64,96},{96,128},{128,160},{160,192},{192,224},{224... | collective-permute-start | bytes 78008 | tf_op jit(solution)/shard_map/ppermute | solution.py:21
  86.5 3.9 %collective-permute-start.7 = (f32[5,1,10,130]{3,2,1,0:T(8,128)S(1)}, f32[5,1,10,130]{3,2,1,0:T(8,128)S(1)}, u32[]{:S(2)}, u32[]{:S(2)}) collective-permute-start(f32[5,1,10,130]{3,2,1,0:T(8,128)S(1)} %get-tuple-element.209), channel_id=1, source_target_pairs={{32,0},{64,32},{96,64},{128,96},{160,128},{192,160},{224,192},{0,2... | collective-permute-start | bytes 78008 | tf_op jit(solution)/shard_map/ppermute | solution.py:24
  90.6 6.5 %collective-permute-start.8 = (f32[5,12,1,130]{3,2,1,0:T(1,128)S(1)}, f32[5,12,1,130]{3,2,1,0:T(1,128)S(1)}, u32[]{:S(2)}, u32[]{:S(2)}) collective-permute-start(f32[5,12,1,130]{3,2,1,0:T(1,128)S(1)} %get-tuple-element.205), channel_id=1, source_target_pairs={{0,4},{4,8},{8,12},{12,16},{16,20},{20,24},{24,28},{28,0},{1,5},{5... | collective-permute-start | bytes 93608 | tf_op jit(solution)/shard_map/ppermute | solution.py:21
  90.7 15.7 %collective-permute-start.9 = (f32[5,12,1,130]{3,2,1,0:T(1,128)S(1)}, f32[5,12,1,130]{3,2,1,0:T(1,128)S(1)}, u32[]{:S(2)}, u32[]{:S(2)}) collective-permute-start(f32[5,12,1,130]{3,2,1,0:T(1,128)S(1)} %get-tuple-element.206), channel_id=1, source_target_pairs={{4,0},{8,4},{12,8},{16,12},{20,16},{24,20},{28,24},{0,28},{5,1},{9... | collective-permute-start | bytes 93608 | tf_op jit(solution)/shard_map/ppermute | solution.py:24
  106.6 16.4 %copy-start.9 = (pred[8]{0:T(512)(128)(4,1)S(1)}, pred[8]{0:T(512)(128)(4,1)}, u32[]{:S(2)}) copy-start(pred[8]{0:T(512)(128)(4,1)} %constant.125.clone.1) | copy-start | bytes 28
  106.8 15.5 %collective-permute-start.10 = (f32[5,12,12,1]{3,2,1,0:T(8,128)S(1)}, f32[5,12,12,1]{3,2,1,0:T(8,128)S(1)}, u32[]{:S(2)}, u32[]{:S(2)}) collective-permute-start(f32[5,12,12,1]{3,2,1,0:T(8,128)S(1)} %get-tuple-element.203), channel_id=1, source_target_pairs={{0,1},{1,2},{2,3},{3,0},{4,5},{5,6},{6,7},{7,4},{8,9},{9,10},{10,1... | collective-permute-start | bytes 8648 | tf_op jit(solution)/shard_map/ppermute | solution.py:21
  106.9 15.4 %collective-permute-start.11 = (f32[5,12,12,1]{3,2,1,0:T(8,128)S(1)}, f32[5,12,12,1]{3,2,1,0:T(8,128)S(1)}, u32[]{:S(2)}, u32[]{:S(2)}) collective-permute-start(f32[5,12,12,1]{3,2,1,0:T(8,128)S(1)} %get-tuple-element.204), channel_id=1, source_target_pairs={{1,0},{2,1},{3,2},{0,3},{5,4},{6,5},{7,6},{4,7},{9,8},{10,9},{11,1... | collective-permute-start | bytes 8648 | tf_op jit(solution)/shard_map/ppermute | solution.py:24
  123.0 0.7 copy-start.11
  123.1 1.2 copy-start.3
  125.4 4.2 %collective-permute-start.12 = (f32[27,1,8,128]{3,2,1,0:T(8,128)S(1)}, f32[27,1,8,128]{3,2,1,0:T(8,128)S(1)}, u32[]{:S(2)}, u32[]{:S(2)}) collective-permute-start(f32[27,1,8,128]{3,2,1,0:T(8,128)S(1)} %get-tuple-element.207), channel_id=1, source_target_pairs={{0,32},{32,64},{64,96},{96,128},{128,160},{160,192},{192,224},{224... | collective-permute-start | bytes 331784 | tf_op jit(solution)/shard_map/ppermute | solution.py:21
  125.4 4.2 %collective-permute-start.13 = (f32[27,1,8,128]{3,2,1,0:T(8,128)S(1)}, f32[27,1,8,128]{3,2,1,0:T(8,128)S(1)}, u32[]{:S(2)}, u32[]{:S(2)}) collective-permute-start(f32[27,1,8,128]{3,2,1,0:T(8,128)S(1)} %get-tuple-element.208), channel_id=1, source_target_pairs={{32,0},{64,32},{96,64},{128,96},{160,128},{192,160},{224,192},{0,2... | collective-permute-start | bytes 331784 | tf_op jit(solution)/shard_map/ppermute | solution.py:24
  129.7 8.8 %collective-permute-start.14 = (f32[27,10,1,128]{3,2,1,0:T(1,128)S(1)}, f32[27,10,1,128]{3,2,1,0:T(1,128)S(1)}, u32[]{:S(2)}, u32[]{:S(2)}) collective-permute-start(f32[27,10,1,128]{3,2,1,0:T(1,128)S(1)} %get-tuple-element.201), channel_id=1, source_target_pairs={{0,4},{4,8},{8,12},{12,16},{16,20},{20,24},{24,28},{28,0},{1,5},{5... | collective-permute-start | bytes 414728 | tf_op jit(solution)/shard_map/ppermute | solution.py:21
  129.8 8.7 %collective-permute-start.15 = (f32[27,10,1,128]{3,2,1,0:T(1,128)S(1)}, f32[27,10,1,128]{3,2,1,0:T(1,128)S(1)}, u32[]{:S(2)}, u32[]{:S(2)}) collective-permute-start(f32[27,10,1,128]{3,2,1,0:T(1,128)S(1)} %get-tuple-element.202), channel_id=1, source_target_pairs={{4,0},{8,4},{12,8},{16,12},{20,16},{24,20},{28,24},{0,28},{5,1},{9... | collective-permute-start | bytes 414728 | tf_op jit(solution)/shard_map/ppermute | solution.py:24
  138.5 5.8 %copy-start.1 = (f32[27,10,1,128]{3,2,1,0:T(1,128)}, f32[27,10,1,128]{3,2,1,0:T(1,128)S(1)}, u32[]{:S(2)}) copy-start(f32[27,10,1,128]{3,2,1,0:T(1,128)S(1)} %collective-permute-done.15) | copy-start | bytes 414724
  146.8 12.8 %collective-permute-start.16 = (f32[27,10,10,1]{0,3,2,1:T(1,128)S(1)}, f32[27,10,10,1]{0,3,2,1:T(1,128)}, u32[]{:S(2)}, u32[]{:S(2)}) collective-permute-start(f32[27,10,10,1]{0,3,2,1:T(1,128)S(1)} %copy.236), channel_id=1, source_target_pairs={{1,0},{2,1},{3,2},{0,3},{5,4},{6,5},{7,6},{4,7},{9,8},{10,9},{11,1... | collective-permute-start | bytes 32408 | tf_op jit(solution)/shard_map/ppermute | solution.py:24
  150.5 6.3 %collective-permute-start.17 = (f32[27,10,10,1]{0,3,2,1:T(1,128)S(1)}, f32[27,10,10,1]{0,3,2,1:T(1,128)}, u32[]{:S(2)}, u32[]{:S(2)}) collective-permute-start(f32[27,10,10,1]{0,3,2,1:T(1,128)S(1)} %copy.238), channel_id=1, source_target_pairs={{0,1},{1,2},{2,3},{3,0},{4,5},{5,6},{6,7},{7,4},{8,9},{9,10},{10,1... | collective-permute-start | bytes 32408 | tf_op jit(solution)/shard_map/ppermute | solution.py:21
  163.6 1.0 copy-start.2
  164.5 1.6 copy-start
  167.9 0.9 copy-start.10
where the time goes:
time: 170 us; the launch traced here: 169 us
  waiting for transfers between devices  58.1 us (34%)
  starting transfers between devices  33.7 us (20%)
  matrix products  30.6 us (18%)
  other arithmetic  23.8 us (14%)
  local copies, waits for them, and re-layouts  19.3 us (11%)
  between operations  2.02 us (1%)
    ppermute x9, waiting for transfers between devices, with_halo(): lax.ppermute(lax.slice_in_dim(block, block.shape[dim] - width, None, axis...  42.2 us
    ppermute x9, starting transfers between devices, with_halo(): lax.ppermute(lax.slice_in_dim(block, 0, width, axis=dim), axis, backward)  28.5 us
    dot_general x16, matrix products, tile_step(): jnp.einsum('cxyp,zp->cxyz', spread_load, weight_z, precision=lax.Precisio...  17.5 us
    ppermute x9, waiting for transfers between devices, with_halo(): lax.ppermute(lax.slice_in_dim(block, 0, width, axis=dim), axis, backward)  15.9 us
    dot_general x16, matrix products, tile_step(): jnp.einsum('cxyz,zp->cxyp', rimmed, weight_z, precision=lax.Precision.HIG...  13.1 us
    broadcast_in_dim x16, other arithmetic, parcel_exchange_parts(): thermal_exchange[None]  12.6 us
    unnamed x54, other arithmetic  6.81 us
    slice x7, local copies, waits for them, and re-layouts, with_halo(): lax.slice_in_dim(block, block.shape[dim] - width, None, axis=dim)  5.83 us
  transfers between devices with their start and end apart: 18, of which 11 were waited for; matrix products, arithmetic and copies ran while one was open for 2% of the time, Pallas kernels for 0%

commit v1 on v0

v1 whole, which is shorter than its diff:
```python
import functools

import jax
import jax.numpy as jnp
from jax import lax
from jax.experimental import pallas as pl
from jax.experimental.pallas import tpu as pltpu
from jax.sharding import PartitionSpec as P

AXES = ("gx", "gy", "gz")
CHUNK = 256
PARCELS = 2048
PITCH = 24
F32 = jnp.float32
BF16 = jnp.bfloat16


def step_of(q):
    return q // 9 - 1, q // 3 % 3 - 1, q % 3 - 1


def weight_of(q):
    value = 1.0
    for step in step_of(q):
        value = value * (2.0 / 3.0 if step == 0 else 1.0 / 6.0)
    return value


def roll(v, k):
    k = k % 128
    return pltpu.roll(v, k, 1) if k else v


def split(v):
    hi = v.astype(BF16)
    lo = (v - hi.astype(F32)).astype(BF16)
    return hi, lo


def side_index(dx, dy):
    return 3 * (dx + 1) + dy + 1


Y_UP = [9 * a + 6 + b for a in range(3) for b in range(3)]
Y_DOWN = [9 * a + b for a in range(3) for b in range(3)]


def kernel(
    f, gt, gv, base, frac, vel, temp, rate, live,
    fo, to, vo, mo,
    ext, rho, ysend, csend, crecv, zsend, zrecv,
    a4, amat, bmat, dep, rim,
    dxr, dyr, c2send, c2recv, z2send, z2recv,
    pop, y3send, y3recv, c3send, c3recv, z3send, z3recv, zcol,
    send_sem, recv_sem,
):
    me = [lax.axis_index(a) for a in AXES]
    size = [lax.axis_size(a) for a in AXES]

    def device(d):
        return tuple(
            me[i] if d[i] == 0 else lax.rem(me[i] + (d[i] + size[i]), size[i]) for i in range(3)
        )

    around = [
        (dx, dy, dz)
        for dz in (-1, 1, 0)
        for dx in (-1, 0, 1)
        for dy in (-1, 0, 1)
        if (dx, dy, dz) != (0, 0, 0)
    ]
    barrier = pltpu.get_barrier_semaphore()
    for d in around:
        pl.semaphore_signal(
            barrier, inc=1, device_id=device(d), device_id_type=pl.DeviceIdType.MESH
        )

    def exchange(phase, moves):
        copies = []
        for n, (src, dst, d) in enumerate(moves):
            copy = pltpu.make_async_remote_copy(
                src_ref=src,
                dst_ref=dst,
                send_sem=send_sem.at[phase, n],
                recv_sem=recv_sem.at[phase, n],
                device_id=device(d),
                device_id_type=pl.DeviceIdType.MESH,
            )
            copy.start()
            copies.append(copy)
        return copies

    lane = lax.broadcasted_iota(jnp.int32, (8, 128), 1)
    sub = lax.broadcasted_iota(jnp.int32, (8, 128), 0)

    def skew(v, amount):
        for bit in range(3):
            v = jnp.where((sub >> bit) & 1 == 1, roll(v, amount << bit), v)
        return v

    def spread_row(v, row):
        return jnp.broadcast_to(v[row : row + 1], (8, 128))

    def moment_step(x, _):
        at = pl.multiple_of(x * 40, 8)
        pops = [f[q, x] for q in range(27)]
        total = pops[0]
        for q in range(1, 27):
            total = total + pops[q]
        rho[x] = total
        for axis in range(3):
            up = None
            for q in range(27):
                e = step_of(q)[axis]
                if e == 1:
                    up = pops[q] if up is None else up + pops[q]
                elif e == -1:
                    up = -pops[q] if up is None else up - pops[q]
            ext[pl.ds(at + 8 * axis, 8), :] = up / total
        ext[pl.ds(at + 24, 8), :] = gt[x]
        ext[pl.ds(at + 32, 8), :] = gv[x]
        return 0

    lax.fori_loop(0, 8, moment_step, 0)
    ext[pl.ds(520, 8), :] = jnp.zeros((8, 128), F32)

    for c in range(5):
        for side in range(2):
            ysend[side, pl.ds(8 * c, 8), :] = ext[pl.ds(8 * c + 7 * side, 8, stride=40), :]
    for j in range(4):
        x, y = (7, 0)[j // 2], (7, 0)[j % 2]
        csend[j, pl.ds(0, 5), :] = ext[pl.ds(40 * x + y, 5, stride=8), :]
        csend[j, pl.ds(5, 3), :] = jnp.zeros((3, 128), F32)
    low = jnp.zeros((8, 128), F32)
    high = jnp.zeros((8, 128), F32)
    for x in range(8):
        for c in range(5):
            at = 8 * x + c
            turned = roll(ext[pl.ds(8 * (5 * x + c), 8), :], at + 1)
            high = jnp.where(lane == at, turned, high)
            low = jnp.where(lane == at + 1, turned, low)
    zsend[0] = low
    zsend[1] = high

    pl.semaphore_wait(barrier, 26)

    def z_moves(send, recv):
        return [
            (
                send.at[(1 + dz) // 2],
                recv.at[(1 - dz) // 2, side_index(-dx, -dy)],
                (dx, dy, dz),
            )
            for (dx, dy, dz) in around
            if dz != 0
        ]

    def corner_moves(send, recv):
        return [
            (send.at[j], recv.at[j], ((1, -1)[j // 2], (1, -1)[j % 2], 0)) for j in range(4)
        ]

    copies1 = exchange(
        0,
        z_moves(zsend, zrecv)
        + [
            (ext.at[pl.ds(280, 40)], ext.at[pl.ds(320, 40)], (1, 0, 0)),
            (ext.at[pl.ds(0, 40)], ext.at[pl.ds(360, 40)], (-1, 0, 0)),
            (ysend.at[1], ext.at[pl.ds(400, 40)], (0, 1, 0)),
            (ysend.at[0], ext.at[pl.ds(440, 40)], (0, -1, 0)),
        ]
        + corner_moves(csend, crecv),
    )

    def collide_step(x, _):
        at = pl.multiple_of(x * 40, 8)
        to_row = pl.multiple_of(PITCH * (x + 1) + 8, 8)
        u = [ext[pl.ds(at + 8 * axis, 8), :] for axis in range(3)]
        speed = u[0] * u[0] + u[1] * u[1] + u[2] * u[2]
        total = rho[x]
        rest = 1.0 - 1.5 * speed
        for q in range(27):
            e = step_of(q)
            along = None
            for axis in range(3):
                if e[axis] != 0:
                    term = u[axis] if e[axis] == 1 else -u[axis]
                    along = term if along is None else along + term
            inner = rest if along is None else rest + along * (3.0 + 4.5 * along)
            equil = (1.25 * weight_of(q)) * total * inner
            pop[q, pl.ds(to_row, 8), :] = equil - 0.25 * f[q, x]
        return 0

    lax.fori_loop(0, 8, collide_step, 0)
    dep[...] = jnp.zeros_like(dep)
    rim[...] = jnp.zeros_like(rim)
    bmat[pl.ds(432, 80), :] = jnp.zeros((80, CHUNK), BF16)

    for copy in copies1:
        copy.wait_recv()

    for j in range(4):
        ext[pl.ds(480 + j, 5, stride=8), :] = crecv[j, pl.ds(0, 5), :]
    for c in range(5):
        ext[pl.ds(480 + 8 * c + 4, 4), :] = jnp.zeros((4, 128), F32)

    columns = []
    for s in range(13):
        sides = []
        for side in range(2):
            to_lane = 8 * side - side
            if s < 8:
                t = roll(zrecv[side, side_index(0, 0)], to_lane - 8 * s)
            elif s < 10:
                dx = (-1, 1)[s - 8]
                t = roll(zrecv[side, side_index(dx, 0)], to_lane - (56, 0)[s - 8])
            elif s < 12:
                dy = (-1, 1)[s - 10]
                t = spread_row(zrecv[side, side_index(0, dy)], (7, 0)[s - 10])
                t = skew(roll(t, to_lane), -8)
            else:
                t = jnp.zeros((8, 128), F32)
                for j in range(4):
                    got = zrecv[side, side_index((-1, 1)[j // 2], (-1, 1)[j % 2])]
                    got = roll(got, to_lane - (56, 0)[j // 2])
                    t = jnp.where(sub == j, spread_row(got, (7, 0)[j % 2]), t)
            sides.append(t)
        both = jnp.where(lane < 8, sides[0], jnp.where(lane < 16, sides[1], 0.0))
        hi = both.astype(BF16).astype(F32)
        both = hi + roll(both - hi, 16) + roll(hi, 32)
        for c in range(5):
            a4[pl.ds(8 * (5 * s + c), 8), :] = jnp.where(
                ((lane & 7) == c) & (lane < 48), both, 0.0
            )
    a4[pl.ds(520, 8), :] = jnp.zeros((8, 128), F32)

    def matrix_step(n, _):
        at = pl.multiple_of(n * 16, 16)
        hi, lo = split(ext[pl.ds(at, 16), :])
        amat[pl.ds(at, 16), pl.ds(0, 128)] = hi
        amat[pl.ds(at, 16), pl.ds(128, 128)] = hi
        amat[pl.ds(at, 16), pl.ds(256, 128)] = lo
        amat[pl.ds(at, 16), pl.ds(384, 128)] = a4[pl.ds(at, 16), :].astype(BF16)
        return 0

    lax.fori_loop(0, 33, matrix_step, 0)

    alive = live[0]

    def chunk_step(n, _):
        first = pl.multiple_of(n * CHUNK, CHUNK)
        here = pl.ds(first, CHUNK)
        bx, by, bz = (base[d : d + 1, here] for d in range(3))
        fx, fy, fz = (frac[d : d + 1, here] for d in range(3))
        rows8 = lax.broadcasted_iota(jnp.int32, (8, CHUNK), 0)

        def hat(cells, b, fr):
            return jnp.where(cells == b, 1.0 - fr, jnp.where(cells == b + 1, fr, 0.0))

        wz = hat(lax.broadcasted_iota(jnp.int32, (128, CHUNK), 0), bz, fz)
        wz_hi, wz_lo = split(wz)
        bmat[pl.ds(0, 128), :] = wz_hi
        bmat[pl.ds(128, 128), :] = wz_lo
        bmat[pl.ds(256, 128), :] = wz_hi
        below = jnp.where(bz == -1, 1.0 - fz, 0.0)
        above = jnp.where(bz == 127, fz, 0.0)
        rows16 = lax.broadcasted_iota(jnp.int32, (16, CHUNK), 0)
        rim_hi, rim_lo = split(jnp.where(rows16 < 8, below, above))
        bmat[pl.ds(384, 16), :] = rim_hi
        bmat[pl.ds(400, 16), :] = rim_hi
        bmat[pl.ds(416, 16), :] = rim_lo

        wx8 = hat(rows8, bx, fx)
        wy8 = hat(rows8, by, fy)
        x_low = jnp.where(bx == -1, 1.0 - fx, 0.0)
        x_high = jnp.where(bx == 7, fx, 0.0)
        y_low = jnp.where(by == -1, 1.0 - fy, 0.0)
        y_high = jnp.where(by == 7, fy, 0.0)
        plane = [wx8[x : x + 1] * wy8 for x in range(8)]
        plane += [x_low * wy8, x_high * wy8, y_low * wx8, y_high * wx8]
        edge = jnp.where(rows8 < 2, x_low, x_high) * jnp.where((rows8 & 1) == 0, y_low, y_high)
        plane.append(jnp.where(rows8 < 4, edge, 0.0))

        along = jnp.dot(amat[...], bmat[...], preferred_element_type=F32)
        sampled = []
        for c in range(5):
            total = None
            for s in range(13):
                at = 8 * (5 * s + c)
                term = along[at : at + 8] * plane[s]
                total = term if total is None else total + term
            sampled.append(jnp.sum(total, axis=0, keepdims=True))

        slot = lax.broadcasted_iota(jnp.int32, (1, CHUNK), 1) + first
        alive_here = slot < alive
        factor = jnp.where(alive_here, rate[0:1, here], 0.0)
        own_temp = temp[0:1, here]
        terms = []
        for d in range(3):
            motion = vel[d : d + 1, here]
            change = factor * (sampled[d] - motion)
            mo[d : d + 1, here] = motion + change
            terms.append(-2.0 * change)
        terms.append(factor * (own_temp - sampled[3]))
        terms.append(factor * (0.05 * jnp.exp(3.0 * (own_temp - 0.5)) - sampled[4]))

        load = [plane[s] * terms[c] for s in range(13) for c in range(5)]
        load.append(jnp.zeros((8, CHUNK), F32))
        load_hi, load_lo = split(jnp.concatenate(load, axis=0))
        nt = (((1,), (1,)), ((), ()))
        wz_both = bmat[pl.ds(0, 256), :]
        got_hi = lax.dot_general(load_hi, wz_both, nt, preferred_element_type=F32)
        got_lo = lax.dot_general(load_lo, wz_hi, nt, preferred_element_type=F32)
        dep[...] += got_hi[:, :128] + got_hi[:, 128:] + got_lo

        plane_hi, plane_lo = split(
            jnp.concatenate(plane + [jnp.zeros((24, CHUNK), F32)], axis=0)
        )
        rows = []
        zero3 = jnp.zeros((3, CHUNK), F32)
        stacked = jnp.concatenate(terms + [zero3], axis=0)
        side_hi, side_lo = split(jnp.concatenate([stacked * below, stacked * above], axis=0))
        plane_both = jnp.concatenate([plane_hi, plane_lo], axis=0)
        edge_hi = lax.dot_general(side_hi, plane_both, nt, preferred_element_type=F32)
        edge_lo = lax.dot_general(side_lo, plane_hi, nt, preferred_element_type=F32)
        rim[pl.ds(0, 16), :] += edge_hi[:, :128] + edge_hi[:, 128:] + edge_lo
        return 0

    lax.fori_loop(0, PARCELS // CHUNK, chunk_step, 0)

    by_row = jnp.transpose(rim[...])
    low = jnp.zeros((8, 128), F32)
    high = jnp.zeros((8, 128), F32)
    for s in range(13):
        v = by_row[8 * s : 8 * s + 8]
        mine = (lane >> 3) == s
        low = jnp.where(mine, roll(v, 8 * s), low)
        high = jnp.where(mine, roll(v, 8 * s - 8), high)
    z2send[0] = low
    z2send[1] = high
    for j in range(4):
        c2send[j, pl.ds(0, 5), :] = dep[pl.ds(480 + 3 - j, 5, stride=8), :]
        c2send[j, pl.ds(5, 3), :] = jnp.zeros((3, 128), F32)
    copies2 = exchange(
        1,
        z_moves(z2send, z2recv)
        + [
            (dep.at[pl.ds(360, 40)], dxr.at[0], (1, 0, 0)),
            (dep.at[pl.ds(320, 40)], dxr.at[1], (-1, 0, 0)),
            (dep.at[pl.ds(440, 40)], dyr.at[0], (0, 1, 0)),
            (dep.at[pl.ds(400, 40)], dyr.at[1], (0, -1, 0)),
        ]
        + corner_moves(c2send, c2recv),
    )
    for copy in copies2:
        copy.wait_recv()

    ends = []
    for side in range(2):
        acc = jnp.where(lane < 64, z2recv[side, side_index(0, 0)], 0.0)
        acc += jnp.where(lane < 8, roll(z2recv[side, side_index(-1, 0)], -72), 0.0)
        acc += jnp.where((lane >> 3) == 7, roll(z2recv[side, side_index(1, 0)], -8), 0.0)
        for dy, from_slot, row in ((-1, 11, 0), (1, 10, 7)):
            t = roll(z2recv[side, side_index(0, dy)], -8 * from_slot)
            t = skew(jnp.where(lane < 8, t, 0.0), 8)
            acc += jnp.where(sub == row, jnp.sum(t, axis=0, keepdims=True), 0.0)
        for j in range(4):
            dx, dy = (-1, 1)[j // 2], (-1, 1)[j % 2]
            to_x, row = (0, 7)[j // 2], (0, 7)[j % 2]
            t = roll(z2recv[side, side_index(dx, dy)], 8 * to_x - 96)
            t = spread_row(t, 3 - j)
            acc += jnp.where((sub == row) & ((lane >> 3) == to_x), t, 0.0)
        ends.append(acc)

    for x in range(8):
        for c in range(5):
            at = 8 * (5 * x + c)
            k = 8 * x + c
            v = dep[pl.ds(at, 8), :]
            v += jnp.where(lane == 0, roll(ends[0], -k), 0.0)
            v += jnp.where(lane == 127, roll(ends[1], 127 - k), 0.0)
            top = dyr[0, pl.ds(8 * c + x, 1), :]
            bottom = dyr[1, pl.ds(8 * c + x, 1), :]
            if x == 0:
                v += dxr[0, pl.ds(8 * c, 8), :]
                top += c2recv[0, pl.ds(c, 1), :]
                bottom += c2recv[1, pl.ds(c, 1), :]
            if x == 7:
                v += dxr[1, pl.ds(8 * c, 8), :]
                top += c2recv[2, pl.ds(c, 1), :]
                bottom += c2recv[3, pl.ds(c, 1), :]
            v += jnp.where(sub == 0, top, 0.0) + jnp.where(sub == 7, bottom, 0.0)
            rho_at = v
            a4[pl.ds(at, 8), :] = rho_at

    def push_step(x, _):
        at = pl.multiple_of(x * 40, 8)
        to_row = pl.multiple_of(PITCH * (x + 1) + 8, 8)
        s = [a4[pl.ds(at + 8 * c, 8), :] for c in range(5)]
        to[x] = gt[x] + s[3]
        vo[x] = gv[x] + s[4]
        for q in range(27):
            e = step_of(q)
            push = s[4]
            for axis in range(3):
                if e[axis] == 1:
                    push = push + 3.0 * s[axis]
                elif e[axis] == -1:
                    push = push - 3.0 * s[axis]
            pop[q, pl.ds(to_row, 8), :] += weight_of(q) * push
        return 0

    lax.fori_loop(0, 8, push_step, 0)

    for k in range(9):
        y3send[0, pl.ds(8 * k, 8), :] = pop[Y_DOWN[k], pl.ds(PITCH + 8, 8, stride=PITCH), :]
        y3send[1, pl.ds(8 * k, 8), :] = pop[Y_UP[k], pl.ds(PITCH + 15, 8, stride=PITCH), :]
    for j in range(4):
        sx, sy = (1, -1)[j // 2], (1, -1)[j % 2]
        row = PITCH * ((7, 0)[j // 2] + 1) + 8 + (7, 0)[j % 2]
        for k in range(3):
            q = 9 * (sx + 1) + 3 * (sy + 1) + k
            c3send[j, pl.ds(k, 1), :] = pop[q, pl.ds(row, 1), :]
        c3send[j, pl.ds(3, 5), :] = jnp.zeros((5, 128), F32)
    low = jnp.zeros((8, 128), F32)
    high = jnp.zeros((8, 128), F32)
    for x in range(8):
        for m in range(9):
            at = 16 * x + m
            row = PITCH * (x + 1) + 8
            low = jnp.where(lane == at, roll(pop[3 * m, pl.ds(row, 8), :], at), low)
            high = jnp.where(lane == at, roll(pop[3 * m + 2, pl.ds(row, 8), :], at + 1), high)
    z3send[0] = low
    z3send[1] = high
    copies3 = exchange(
        2,
        z_moves(z3send, z3recv)
        + [
            (
                pop.at[pl.ds(18, 9), pl.ds(PITCH * 8 + 8, 8)],
                pop.at[pl.ds(18, 9), pl.ds(8, 8)],
                (1, 0, 0),
            ),
            (
                pop.at[pl.ds(0, 9), pl.ds(PITCH + 8, 8)],
                pop.at[pl.ds(0, 9), pl.ds(PITCH * 9 + 8, 8)],
                (-1, 0, 0),
            ),
            (y3send.at[1], y3recv.at[0], (0, 1, 0)),
            (y3send.at[0], y3recv.at[1], (0, -1, 0)),
        ]
        + corner_moves(c3send, c3recv),
    )
    for copy in copies3:
        copy.wait_recv()

    for k in range(9):
        pop[Y_UP[k], pl.ds(PITCH + 7, 8, stride=PITCH), :] = y3recv[0, pl.ds(8 * k, 8), :]
        pop[Y_DOWN[k], pl.ds(PITCH + 16, 8, stride=PITCH), :] = y3recv[1, pl.ds(8 * k, 8), :]
    for j in range(4):
        sx, sy = (1, -1)[j // 2], (1, -1)[j % 2]
        row = PITCH * (0, 9)[j // 2] + (7, 16)[j % 2]
        for k in range(3):
            q = 9 * (sx + 1) + 3 * (sy + 1) + k
            pop[q, pl.ds(row, 1), :] = c3recv[j, pl.ds(k, 1), :]
    for side in range(2):
        face = z3recv[side, side_index(0, 0)]
        for x in range(8):
            zcol[side, pl.ds(PITCH * (x + 1) + 8, 8), :] = roll(face, -16 * x)
        left = z3recv[side, side_index(-1, 0)]
        zcol[side, pl.ds(8, 8), :] = roll(left, -112)
        zcol[side, pl.ds(PITCH * 9 + 8, 8), :] = z3recv[side, side_index(1, 0)]
        t = skew(spread_row(z3recv[side, side_index(0, -1)], 7), -16)
        zcol[side, pl.ds(PITCH + 7, 8, stride=PITCH), :] = t
        t = skew(spread_row(z3recv[side, side_index(0, 1)], 0), -16)
        zcol[side, pl.ds(PITCH + 16, 8, stride=PITCH), :] = t
        for j in range(4):
            t = z3recv[side, side_index((-1, 1)[j // 2], (-1, 1)[j % 2])]
            t = roll(t, (-112, 0)[j // 2])
            row = (7, 0)[j % 2]
            to_row = PITCH * (0, 9)[j // 2] + (7, 16)[j % 2]
            zcol[side, pl.ds(to_row, 1), :] = t[row : row + 1]

    for q in range(27):
        ex, ey, ez = step_of(q)
        m = q // 3
        for x in range(8):
            row = PITCH * (x - ex + 1) + 8 - ey
            v = pop[q, pl.ds(row, 8), :]
            if ez == 1:
                v = jnp.where(lane == 0, roll(zcol[0, pl.ds(row, 8), :], -m), roll(v, 1))
            elif ez == -1:
                v = jnp.where(lane == 127, roll(zcol[1, pl.ds(row, 8), :], 127 - m), roll(v, -1))
            fo[q, x] = v

    for copies in (copies1, copies2, copies3):
        for copy in copies:
            copy.wait_send()


def on_device(f, gt, gv, base, frac, vel, temp, rate, live):
    vmem = pl.BlockSpec(memory_space=pltpu.VMEM)
    fo, to, vo, mo = pl.pallas_call(
        kernel,
        out_shape=(
            jax.ShapeDtypeStruct(f.shape, F32),
            jax.ShapeDtypeStruct(gt.shape, F32),
            jax.ShapeDtypeStruct(gv.shape, F32),
            jax.ShapeDtypeStruct((3, PARCELS), F32),
        ),
        in_specs=[vmem] * 8 + [pl.BlockSpec(memory_space=pltpu.SMEM)],
        out_specs=[vmem] * 4,
        scratch_shapes=[
            pltpu.VMEM((528, 128), F32),
            pltpu.VMEM((8, 8, 128), F32),
            pltpu.VMEM((2, 40, 128), F32),
            pltpu.VMEM((4, 8, 128), F32),
            pltpu.VMEM((4, 8, 128), F32),
            pltpu.VMEM((2, 8, 128), F32),
            pltpu.VMEM((2, 9, 8, 128), F32),
            pltpu.VMEM((528, 128), F32),
            pltpu.VMEM((528, 512), BF16),
            pltpu.VMEM((512, CHUNK), BF16),
            pltpu.VMEM((528, 128), F32),
            pltpu.VMEM((128, 128), F32),
            pltpu.VMEM((2, 40, 128), F32),
            pltpu.VMEM((2, 40, 128), F32),
            pltpu.VMEM((4, 8, 128), F32),
            pltpu.VMEM((4, 8, 128), F32),
            pltpu.VMEM((2, 8, 128), F32),
            pltpu.VMEM((2, 9, 8, 128), F32),
            pltpu.VMEM((27, 10 * PITCH, 128), F32),
            pltpu.VMEM((2, 72, 128), F32),
            pltpu.VMEM((2, 72, 128), F32),
            pltpu.VMEM((4, 8, 128), F32),
            pltpu.VMEM((4, 8, 128), F32),
            pltpu.VMEM((2, 8, 128), F32),
            pltpu.VMEM((2, 9, 8, 128), F32),
            pltpu.VMEM((2, 10 * PITCH, 128), F32),
            pltpu.SemaphoreType.DMA((3, 26)),
            pltpu.SemaphoreType.DMA((3, 26)),
        ],
        compiler_params=pltpu.CompilerParams(
            collective_id=0, has_side_effects=True, vmem_limit_bytes=40 * 1024 * 1024
        ),
    )(
        f,
        gt,
        gv,
        base.reshape(3, PARCELS),
        frac.reshape(3, PARCELS),
        vel.reshape(3, PARCELS),
        temp.reshape(1, PARCELS),
        rate.reshape(1, PARCELS),
        live.reshape(1),
    )
    return fo, to, vo, mo.reshape(vel.shape)


def solution(mesh):
    placed = (
        P(None, "gx", "gy", "gz"),
        P("gx", "gy", "gz"),
        P("gx", "gy", "gz"),
        P(None, "gx", "gy", "gz", None),
        P(None, "gx", "gy", "gz", None),
        P(None, "gx", "gy", "gz", None),
        P("gx", "gy", "gz", None),
        P("gx", "gy", "gz", None),
        P("gx", "gy", "gz"),
    )
    return jax.shard_map(
        on_device,
        mesh=mesh,
        in_specs=placed,
        out_specs=(
            P(None, "gx", "gy", "gz"),
            P("gx", "gy", "gz"),
            P("gx", "gy", "gz"),
            P(None, "gx", "gy", "gz", None),
        ),
        check_vma=False,
    )
```

time: 170 us -> 45.8 us (0.27)
  the two profiles are of different devices: /device:TPU:24 before, /device:TPU:1 now
where the time goes in v1:
time: 45.8 us; the launch traced here: 45.5 us
  Pallas kernels  38.7 us (84%)
  local copies, waits for them, and re-layouts  5.46 us (12%)
  between operations  1.36 us (3%)
    pallas_call x1, Pallas kernels, on_device(): pl.pallas_call(kernel, out_shape=(jax.ShapeDtypeStruct(f.shape, F32), jax...  38.7 us
    unnamed x20, local copies, waits for them, and re-layouts  5.46 us

profile of v1, /device:TPU:1, one launch (start us, length us, event | category | flops | bytes accessed | tf_op | source)
XLA Modules:
  0.0 45.5 jit_solution(13627040488892140308)
XLA Ops:
  1.3 0.0 copy-start.5
  1.3 0.0 copy-start.6
  1.3 0.8 %copy.20 = s32[3,1,1,1,2048]{4,0,2,1,3:T(4,128)S(1)} copy(s32[3,1,1,1,2048]{4,3,2,1,0:T(1,128)} %param.12) | data formatting | bytes 49152
  2.1 0.0 copy-done.5
  2.1 0.0 copy-done.6
  2.1 0.0 copy-start.1
  2.1 0.0 copy-start.2
  2.1 0.0 copy-start.3
  2.1 0.0 copy-start.4
  2.2 0.7 %copy-done.1 = f32[8,8,128]{2,1,0:T(8,128)S(1)} copy-done((f32[8,8,128]{2,1,0:T(8,128)S(1)}, f32[8,8,128]{2,1,0:T(8,128)}, u32[]{:S(2)}) %copy-start.1) | copy-done | bytes 32792
  2.8 0.0 copy-done.2
  2.9 0.0 copy-done.3
  2.9 0.0 copy-done.4
  2.9 0.0 copy-start
  2.9 1.2 %copy-done = f32[27,8,8,128]{3,2,1,0:T(8,128)S(1)} copy-done((f32[27,8,8,128]{3,2,1,0:T(8,128)S(1)}, f32[27,8,8,128]{3,2,1,0:T(8,128)}, u32[]{:S(2)}) %copy-start) | copy-done | bytes 884760
  4.0 38.7 %shard_map.120 = (f32[27,8,8,128]{3,2,1,0:T(8,128)S(1)}, f32[8,8,128]{2,1,0:T(8,128)S(1)}, f32[8,8,128]{2,1,0:T(8,128)S(1)}, f32[3,2048]{1,0:T(4,128)S(1)}) custom-call(f32[27,8,8,128]{3,2,1,0:T(8,128)S(1)} %copy-done, f32[8,8,128]{2,1,0:T(8,128)S(1)} %copy-done.1, f32[8,8,128]{2,1,0:T(8,128)S(1)} %copy-done.2, s32[3,2048]{1,0:T(4,128)S(1)} %bitcast.12, ...), custom_call_target="tpu_custom_call" | custom-call | tf_op jit(solution)/shard_map/pallas_call | solution.py:503
  42.8 0.6 %copy.13 = f32[3,1,1,1,2048]{4,3,2,1,0:T(1,128)} copy(f32[3,1,1,1,2048]{4,0,3,2,1:T(4,128)S(1)} %bitcast.13) | data formatting | bytes 49152
  43.4 0.9 %copy.25 = f32[27,8,8,128]{3,2,1,0:T(8,128)} copy(f32[27,8,8,128]{3,2,1,0:T(8,128)S(1)} %get-tuple-element.22) | data formatting | bytes 1769472
  44.3 0.6 %copy.26 = f32[8,8,128]{2,1,0:T(8,128)} copy(f32[8,8,128]{2,1,0:T(8,128)S(1)} %get-tuple-element.23) | data formatting | bytes 65536
  44.9 0.6 %copy.27 = f32[8,8,128]{2,1,0:T(8,128)} copy(f32[8,8,128]{2,1,0:T(8,128)S(1)} %get-tuple-element.24) | data formatting | bytes 65536
  (1 shorter events, 0.0 us)
Async XLA Ops:
  1.3 0.8 %copy-start.5 = (f32[3,1,1,1,2048]{4,3,2,1,0:T(1,128)S(1)}, f32[3,1,1,1,2048]{4,3,2,1,0:T(1,128)}, u32[]{:S(2)}) copy-start(f32[3,1,1,1,2048]{4,3,2,1,0:T(1,128)} %param.14) | copy-start | bytes 73732
  1.3 0.8 %copy-start.6 = (f32[3,1,1,1,2048]{4,3,2,1,0:T(1,128)S(1)}, f32[3,1,1,1,2048]{4,3,2,1,0:T(1,128)}, u32[]{:S(2)}) copy-start(f32[3,1,1,1,2048]{4,3,2,1,0:T(1,128)} %param.13) | copy-start | bytes 73732
  2.1 0.8 %copy-start.1 = (f32[8,8,128]{2,1,0:T(8,128)S(1)}, f32[8,8,128]{2,1,0:T(8,128)}, u32[]{:S(2)}) copy-start(f32[8,8,128]{2,1,0:T(8,128)} %gt.1) | copy-start | bytes 98308
  2.1 0.8 %copy-start.2 = (f32[8,8,128]{2,1,0:T(8,128)S(1)}, f32[8,8,128]{2,1,0:T(8,128)}, u32[]{:S(2)}) copy-start(f32[8,8,128]{2,1,0:T(8,128)} %gv.1) | copy-start | bytes 98308
  2.1 0.8 %copy-start.3 = (f32[1,1,1,2048]{3,2,1,0:T(1,128)S(1)}, f32[1,1,1,2048]{3,2,1,0:T(1,128)}, u32[]{:S(2)}) copy-start(f32[1,1,1,2048]{3,2,1,0:T(1,128)} %param.15) | copy-start | bytes 24580
  2.1 0.7 %copy-start.4 = (f32[1,1,1,2048]{3,2,1,0:T(1,128)S(1)}, f32[1,1,1,2048]{3,2,1,0:T(1,128)}, u32[]{:S(2)}) copy-start(f32[1,1,1,2048]{3,2,1,0:T(1,128)} %param.16) | copy-start | bytes 24580
  2.9 1.2 %copy-start = (f32[27,8,8,128]{3,2,1,0:T(8,128)S(1)}, f32[27,8,8,128]{3,2,1,0:T(8,128)}, u32[]{:S(2)}) copy-start(f32[27,8,8,128]{3,2,1,0:T(8,128)} %f.1) | copy-start | bytes 2654212

commit v2 on v1

v2 whole, which is shorter than its diff:
```python
import jax
import jax.numpy as jnp
from jax import lax
from jax.experimental import pallas as pl
from jax.experimental.pallas import tpu as pltpu
from jax.sharding import PartitionSpec as P

AXES = ("gx", "gy", "gz")
CHUNK = 256
PARCELS = 2048
PITCH = 24
F32 = jnp.float32
BF16 = jnp.bfloat16
MESH = pl.DeviceIdType.MESH
NT = (((1,), (1,)), ((), ()))


def step_of(q):
    return q // 9 - 1, q // 3 % 3 - 1, q % 3 - 1


def weight_of(q):
    value = 1.0
    for step in step_of(q):
        value = value * (2.0 / 3.0 if step == 0 else 1.0 / 6.0)
    return value


def roll(v, k):
    k = k % 128
    return pltpu.roll(v, k, 1) if k else v


def split(v):
    hi = v.astype(BF16)
    lo = (v - hi.astype(F32)).astype(BF16)
    return hi, lo


def side_index(dx, dy):
    return 3 * (dx + 1) + dy + 1


def place_of(x, y):
    if 0 <= x < 8:
        return (x, y) if 0 <= y < 8 else (10 if y < 0 else 11, x)
    if 0 <= y < 8:
        return 8 if x < 0 else 9, y
    return 12, 2 * (x > 0) + (y > 0)


SIGNS = [(1, 1), (1, -1), (-1, 1), (-1, -1)]
Y_UP = [9 * a + 6 + b for a in range(3) for b in range(3)]
Y_DOWN = [9 * a + b for a in range(3) for b in range(3)]


def push_of(q, s):
    push = s[4]
    e = step_of(q)
    for axis in range(3):
        if e[axis] == 1:
            push = push + 3.0 * s[axis]
        elif e[axis] == -1:
            push = push - 3.0 * s[axis]
    return weight_of(q) * push


def gather_kernel(
    f_in, gt_in, gv_in, base_in, frac_in, vel_in, temp_in, rate_in, live,
    fo, to_out, vo_out, mo_out,
    pop, zcol, to, vo, mo, staged,
    f, gt, gv, base, frac, vel, temp, rate,
    ext, ysend, csend, crecv, zsend, zrecv, ybsend, ybrecv, xbrecv,
    amat, wmat, pmat, plane_of, target, factor, sampled, edges,
    dep, rim, zslot, rimf,
    x2send, x2recv, y2send, y2recv, c2send, c2recv, z2send, z2recv, src,
    in_sem, out_sem, send_sem, recv_sem,
):
    me = [lax.axis_index(a) for a in AXES]
    size = [lax.axis_size(a) for a in AXES]

    def device(d):
        return tuple(
            me[i] if d[i] == 0 else lax.rem(me[i] + (d[i] + size[i]), size[i]) for i in range(3)
        )

    around = [
        (dx, dy, dz)
        for dz in (-1, 1, 0)
        for dx in (-1, 1, 0)
        for dy in (-1, 1, 0)
        if (dx, dy, dz) != (0, 0, 0)
    ]
    barrier = pltpu.get_barrier_semaphore()
    for d in around:
        pl.semaphore_signal(barrier, inc=1, device_id=device(d), device_id_type=MESH)

    fetches = []
    for n, (a, b) in enumerate(
        [
            (f_in, f), (gt_in, gt), (gv_in, gv), (base_in, base), (frac_in, frac),
            (vel_in, vel), (temp_in, temp), (rate_in, rate),
        ]
    ):
        fetch = pltpu.make_async_copy(a, b, in_sem.at[n])
        fetch.start()
        fetches.append(fetch)

    def write(pairs, at):
        copies = []
        for n, (a, b) in enumerate(pairs):
            copy = pltpu.make_async_copy(a, b, out_sem.at[at + n])
            copy.start()
            copies.append(copy)
        return copies

    def exchange(phase, moves):
        copies = []
        for n, (a, b, d) in enumerate(moves):
            copy = pltpu.make_async_remote_copy(
                src_ref=a,
                dst_ref=b,
                send_sem=send_sem.at[phase, n],
                recv_sem=recv_sem.at[phase, n],
                device_id=device(d),
                device_id_type=MESH,
            )
            copy.start()
            copies.append(copy)
        return copies

    lane = lax.broadcasted_iota(jnp.int32, (8, 128), 1)
    sub = lax.broadcasted_iota(jnp.int32, (8, 128), 0)
    low_lane = lane & 7
    group = lane >> 3

    def skew(v, amount):
        for bit in range(3):
            v = jnp.where((sub >> bit) & 1 == 1, roll(v, amount << bit), v)
        return v

    def spread_row(v, row):
        return jnp.broadcast_to(v[row : row + 1], (8, 128))

    for fetch in fetches[:3]:
        fetch.wait()

    def moment_step(x, _):
        at = pl.multiple_of(x * 40, 8)
        to_row = pl.multiple_of(PITCH * (x + 1) + 8, 8)
        pops = [f[q, x] for q in range(27)]
        total = pops[0]
        for q in range(1, 27):
            total = total + pops[q]
        u = []
        for axis in range(3):
            up = None
            for q in range(27):
                e = step_of(q)[axis]
                if e == 1:
                    up = pops[q] if up is None else up + pops[q]
                elif e == -1:
                    up = -pops[q] if up is None else up - pops[q]
            u.append(up / total)
            ext[pl.ds(at + 8 * axis, 8), :] = u[axis]
        ext[pl.ds(at + 24, 8), :] = gt[x]
        ext[pl.ds(at + 32, 8), :] = gv[x]
        rest = 1.0 - 1.5 * (u[0] * u[0] + u[1] * u[1] + u[2] * u[2])
        for q in range(27):
            e = step_of(q)
            along = None
            for axis in range(3):
                if e[axis] != 0:
                    term = u[axis] if e[axis] == 1 else -u[axis]
                    along = term if along is None else along + term
            inner = rest if along is None else rest + along * (3.0 + 4.5 * along)
            equil = (1.25 * weight_of(q)) * total * inner
            pop[q, pl.ds(to_row, 8), :] = equil - 0.25 * pops[q]
        return 0

    lax.fori_loop(0, 8, moment_step, 0)

    for c in range(5):
        for side in range(2):
            ysend[side, pl.ds(8 * c, 8), :] = ext[pl.ds(8 * c + 7 * side, 8, stride=40), :]
    for k in range(9):
        ybsend[0, pl.ds(8 * k, 8), :] = pop[Y_DOWN[k], pl.ds(PITCH + 8, 8, stride=PITCH), :]
        ybsend[1, pl.ds(8 * k, 8), :] = pop[Y_UP[k], pl.ds(PITCH + 15, 8, stride=PITCH), :]
    for j, (sx, sy) in enumerate(SIGNS):
        x, y = 7 if sx == 1 else 0, 7 if sy == 1 else 0
        csend[j, pl.ds(0, 5), :] = ext[pl.ds(40 * x + y, 5, stride=8), :]
        for k in range(3):
            q = 9 * (sx + 1) + 3 * (sy + 1) + k
            csend[j, pl.ds(5 + k, 1), :] = pop[q, pl.ds(PITCH * (x + 1) + 8 + y, 1), :]

    def z_pack(x, carry):
        low, high = carry
        at = pl.multiple_of(x * 40, 8)
        row = pl.multiple_of(PITCH * (x + 1) + 8, 8)
        near_low = jnp.zeros((8, 128), F32)
        near_high = jnp.zeros((8, 128), F32)
        for v in range(14):
            if v < 5:
                t_low = t_high = roll(ext[pl.ds(at + 8 * v, 8), :], v + 1)
            else:
                t_low = roll(pop[3 * (v - 5), pl.ds(row, 8), :], v + 1)
                t_high = roll(pop[3 * (v - 5) + 2, pl.ds(row, 8), :], v + 1)
            near_low = jnp.where(lane == v + 1, t_low, near_low)
            near_high = jnp.where(lane == v, t_high, near_high)
        return (
            low + pltpu.roll(near_low, 16 * x, 1),
            high + pltpu.roll(near_high, 16 * x, 1),
        )

    zero8 = jnp.zeros((8, 128), F32)
    low, high = lax.fori_loop(0, 8, z_pack, (zero8, zero8))
    zsend[0] = low
    zsend[1] = high

    for fetch in fetches[3:]:
        fetch.wait()
    alive = live[0]

    def weight_step(n, _):
        first = pl.multiple_of(n * CHUNK, CHUNK)
        here = pl.ds(first, CHUNK)
        bx, by, bz = (base[d, :, here] for d in range(3))
        fx, fy, fz = (frac[d, :, here] for d in range(3))
        rows8 = lax.broadcasted_iota(jnp.int32, (8, CHUNK), 0)

        def hat(cells, b, fr):
            return jnp.where(cells == b, 1.0 - fr, jnp.where(cells == b + 1, fr, 0.0))

        wz_hi, wz_lo = split(hat(lax.broadcasted_iota(jnp.int32, (128, CHUNK), 0), bz, fz))
        wmat[pl.ds(0, 128), here] = wz_hi
        wmat[pl.ds(128, 128), here] = wz_lo
        wmat[pl.ds(256, 128), here] = wz_hi
        edges[pl.ds(0, 1), here] = jnp.where(bz == -1, 1.0 - fz, 0.0)
        edges[pl.ds(1, 1), here] = jnp.where(bz == 127, fz, 0.0)

        wx8 = hat(rows8, bx, fx)
        wy8 = hat(rows8, by, fy)
        x_low = jnp.where(bx == -1, 1.0 - fx, 0.0)
        x_high = jnp.where(bx == 7, fx, 0.0)
        y_low = jnp.where(by == -1, 1.0 - fy, 0.0)
        y_high = jnp.where(by == 7, fy, 0.0)
        plane = [wx8[x : x + 1] * wy8 for x in range(8)]
        plane += [x_low * wy8, x_high * wy8, y_low * wx8, y_high * wx8]
        edge = jnp.where(rows8 < 2, x_low, x_high) * jnp.where((rows8 & 1) == 0, y_low, y_high)
        plane.append(jnp.where(rows8 < 4, edge, 0.0))
        plane = jnp.concatenate(plane + [jnp.zeros((24, CHUNK), F32)], axis=0)
        plane_of[:, here] = plane
        plane_hi, plane_lo = split(plane)
        pmat[pl.ds(0, 128), here] = plane_hi
        pmat[pl.ds(128, 128), here] = plane_lo

        slot = lax.broadcasted_iota(jnp.int32, (1, CHUNK), 1) + first
        own_temp = temp[:, here]
        target[:, here] = jnp.concatenate(
            [vel[d, :, here] for d in range(3)]
            + [own_temp, 0.05 * jnp.exp(3.0 * (own_temp - 0.5)), jnp.zeros((3, CHUNK), F32)],
            axis=0,
        )
        scale = jnp.where(rows8 < 3, 2.0, jnp.where(rows8 < 5, 1.0, 0.0))
        factor[:, here] = jnp.where(slot < alive, rate[:, here], 0.0) * scale
        return 0

    lax.fori_loop(0, PARCELS // CHUNK, weight_step, 0)

    def matrix_step(n, _):
        at = pl.multiple_of(n * 16, 16)
        hi, lo = split(ext[pl.ds(at, 16), :])
        amat[pl.ds(at, 16), pl.ds(0, 128)] = hi
        amat[pl.ds(at, 16), pl.ds(128, 128)] = hi
        amat[pl.ds(at, 16), pl.ds(256, 128)] = lo
        return 0

    pl.semaphore_wait(barrier, 26)

    def z_moves(send, recv):
        return [
            (
                send.at[(1 + dz) // 2],
                recv.at[(1 - dz) // 2, side_index(-dx, -dy)],
                (dx, dy, dz),
            )
            for (dx, dy, dz) in around
            if dz != 0
        ]

    def corner_moves(send, recv):
        return [(send.at[j], recv.at[j], (sx, sy, 0)) for j, (sx, sy) in enumerate(SIGNS)]

    copies1 = exchange(
        0,
        z_moves(zsend, zrecv)
        + corner_moves(csend, crecv)
        + [
            (ysend.at[1], ext.at[pl.ds(400, 40)], (0, 1, 0)),
            (ysend.at[0], ext.at[pl.ds(440, 40)], (0, -1, 0)),
            (ext.at[pl.ds(280, 40)], ext.at[pl.ds(320, 40)], (1, 0, 0)),
            (ext.at[pl.ds(0, 40)], ext.at[pl.ds(360, 40)], (-1, 0, 0)),
            (ybsend.at[1], ybrecv.at[0], (0, 1, 0)),
            (ybsend.at[0], ybrecv.at[1], (0, -1, 0)),
            (pop.at[pl.ds(18, 9), pl.ds(PITCH * 8 + 8, 8)], xbrecv.at[0], (1, 0, 0)),
            (pop.at[pl.ds(0, 9), pl.ds(PITCH + 8, 8)], xbrecv.at[1], (-1, 0, 0)),
        ],
    )

    lax.fori_loop(0, 20, matrix_step, 0)

    def sample(first_slot, last_slot, along, here, off):
        sums = []
        for c in range(5):
            total = None
            for s in range(first_slot, last_slot):
                at = 8 * (5 * s + c) - off
                term = along[at : at + 8] * plane_of[pl.ds(8 * s, 8), here]
                total = term if total is None else total + term
            sums.append(jnp.sum(total, axis=0, keepdims=True))
        return jnp.concatenate(sums + [jnp.zeros((3, CHUNK), F32)], axis=0)

    def own_step(n, _):
        here = pl.ds(pl.multiple_of(n * CHUNK, CHUNK), CHUNK)
        along = jnp.dot(amat[pl.ds(0, 320), :], wmat[:, here], preferred_element_type=F32)
        sampled[:, here] = sample(0, 8, along, here, 0)
        return 0

    lax.fori_loop(0, PARCELS // CHUNK, own_step, 0)
    dep[...] = jnp.zeros_like(dep)
    rim[...] = jnp.zeros_like(rim)

    for copy in copies1:
        copy.wait_recv()

    for j in range(4):
        ext[pl.ds(480 + j, 5, stride=8), :] = crecv[j, pl.ds(0, 5), :]
    for c in range(5):
        ext[pl.ds(480 + 8 * c + 4, 4), :] = jnp.zeros((4, 128), F32)
    ext[pl.ds(520, 8), :] = zero8

    rimf[pl.ds(104, 24), :] = jnp.zeros((24, 128), F32)
    for s in range(13):
        sides = []
        for side in range(2):
            if s < 8:
                t = roll(zrecv[side, side_index(0, 0)], -16 * s - side)
            elif s < 10:
                dx = (-1, 1)[s - 8]
                t = roll(zrecv[side, side_index(dx, 0)], -(112, 0)[s - 8] - side)
            elif s < 12:
                dy = (-1, 1)[s - 10]
                t = spread_row(zrecv[side, side_index(0, dy)], (7, 0)[s - 10])
                t = skew(roll(t, -side), -16)
            else:
                t = zero8
                for j in range(4):
                    got = zrecv[side, side_index((-1, 1)[j // 2], (-1, 1)[j % 2])]
                    got = roll(got, -(112, 0)[j // 2] - side)
                    t = jnp.where(sub == j, spread_row(got, (7, 0)[j % 2]), t)
            zslot[side, pl.ds(8 * s, 8), :] = t
            sides.append(t)
        both = jnp.where(lane < 8, sides[0], roll(sides[1], 8))
        rimf[pl.ds(8 * s, 8), :] = jnp.where((lane < 16) & (low_lane < 5), both, 0.0)
    fields_hi, fields_lo = split(jnp.transpose(rimf[...])[:16])
    rim_left = jnp.concatenate(
        [
            jnp.concatenate([fields_hi, fields_hi], axis=1),
            jnp.concatenate([fields_lo, fields_lo], axis=1),
        ],
        axis=0,
    )

    lax.fori_loop(20, 33, matrix_step, 0)

    def chunk_step(n, _):
        here = pl.ds(pl.multiple_of(n * CHUNK, CHUNK), CHUNK)
        below = edges[pl.ds(0, 1), here]
        above = edges[pl.ds(1, 1), here]
        along = jnp.dot(amat[pl.ds(320, 208), :], wmat[:, here], preferred_element_type=F32)
        got = sampled[:, here] + sample(8, 13, along, here, 320)
        ends = jnp.dot(rim_left, pmat[:, here], preferred_element_type=F32)
        ends = ends[:16] + ends[16:]
        got = got + below * ends[:8] + above * ends[8:]
        terms = factor[:, here] * (target[:, here] - got)
        for d in range(3):
            mo[d, :, here] = target[pl.ds(d, 1), here] - 0.5 * terms[d : d + 1]

        load = [
            plane_of[pl.ds(8 * s, 8), here] * terms[c : c + 1] for s in range(13) for c in range(5)
        ]
        load.append(jnp.zeros((8, CHUNK), F32))
        load_hi, load_lo = split(jnp.concatenate(load, axis=0))
        got_hi = lax.dot_general(
            load_hi, wmat[pl.ds(0, 256), here], NT, preferred_element_type=F32
        )
        got_lo = lax.dot_general(
            load_lo, wmat[pl.ds(0, 128), here], NT, preferred_element_type=F32
        )
        dep[...] += got_hi[:, :128] + got_hi[:, 128:] + got_lo

        side_hi, side_lo = split(jnp.concatenate([terms * below, terms * above], axis=0))
        edge_hi = lax.dot_general(side_hi, pmat[:, here], NT, preferred_element_type=F32)
        edge_lo = lax.dot_general(
            side_lo, pmat[pl.ds(0, 128), here], NT, preferred_element_type=F32
        )
        rim[pl.ds(0, 16), :] += edge_hi[:, :128] + edge_hi[:, 128:] + edge_lo
        return 0

    lax.fori_loop(0, PARCELS // CHUNK, chunk_step, 0)

    by_row = jnp.transpose(rim[...])
    low = zero8
    high = zero8
    for s in range(13):
        v = by_row[8 * s : 8 * s + 8]
        own = [dep[pl.ds(8 * (5 * s + c), 8), :] for c in range(5)]
        mine = group == s
        low = jnp.where(mine, roll(v, 8 * s), low)
        high = jnp.where(mine, roll(v, 8 * s - 8), high)
    ring = jnp.where(
        low_lane == 0,
        roll(low, -4) + 3.0 * roll(low, -2),
        jnp.where(
            low_lane < 3,
            roll(low, 1),
            jnp.where(low_lane == 4, high - 3.0 * roll(high, 2), roll(high, 5)),
        ),
    )
    for s in range(13):
        own = [dep[pl.ds(8 * (5 * s + c), 8), :] for c in range(5)]
        lean = 3.0 * own[2]
        for v, (a, b) in enumerate([(own[4] - lean, own[4] + lean), (own[0],) * 2, (own[1],) * 2]):
            at = 8 * s + 5 + v
            low = jnp.where(lane == at, roll(a, at), low)
            high = jnp.where(lane == at, roll(b, at + 1), high)
    z2send[0] = low
    z2send[1] = high

    def fill(send, blocks, singles, at):
        for n, block in enumerate(blocks):
            send[pl.ds(40 * n, 40), :] = block
        for n, (x, y) in enumerate(singles):
            s, r = place_of(x, y)
            send[pl.ds(at + 8 * n, 5), :] = dep[pl.ds(40 * s + r, 5, stride=8), :]
        send[pl.ds(at + 32, 8), :] = ring

    far = {1: (7, 8), -1: (0, -1)}
    for n, sign in enumerate((-1, 1)):
        a, b = far[sign]
        fill(
            x2send.at[n],
            [dep[pl.ds(40 * place_of(x, 0)[0], 40), :] for x in (a, b)],
            [(a, -1), (a, 8), (b, -1), (b, 8)],
            80,
        )
        for c in range(5):
            y2send[n, pl.ds(8 * c, 8), :] = dep[pl.ds(8 * c + a, 8, stride=40), :]
        y2send[n, pl.ds(40, 40), :] = dep[pl.ds(40 * place_of(0, b)[0], 40), :]
        fill(y2send.at[n], [], [(-1, a), (8, a), (-1, b), (8, b)], 80)
    for j, (sx, sy) in enumerate(SIGNS):
        fill(c2send.at[j], [], [(x, y) for x in far[sx] for y in far[sy]], 0)

    copies2 = exchange(
        1,
        z_moves(z2send, z2recv)
        + corner_moves(c2send, c2recv)
        + [
            (y2send.at[1], y2recv.at[0], (0, 1, 0)),
            (y2send.at[0], y2recv.at[1], (0, -1, 0)),
            (x2send.at[1], x2recv.at[0], (1, 0, 0)),
            (x2send.at[0], x2recv.at[1], (-1, 0, 0)),
        ],
    )
    for copy in copies1:
        copy.wait_send()
    for copy in copies2:
        copy.wait_recv()

    rings = {(0, 0): ring}
    for n, sign in enumerate((-1, 1)):
        rings[sign, 0] = x2recv[n, pl.ds(112, 8), :]
        rings[0, sign] = y2recv[n, pl.ds(112, 8), :]
    for j, (sx, sy) in enumerate(SIGNS):
        rings[-sx, -sy] = c2recv[j, pl.ds(32, 8), :]
    layers = []
    for side in range(2):
        acc = None
        for (dx, dy), ring_at in rings.items():
            t = z2recv[side, side_index(dx, dy)]
            t += jnp.where(low_lane >= 5, roll(ring_at, (5, 1)[side]), 0.0)
            xs = {0: range(-1, 9), -1: (-1, 0), 1: (7, 8)}[dx]
            ys = {0: range(-1, 9), -1: (-1, 0), 1: (7, 8)}[dy]
            singles = [(x, y) for x in xs for y in ys]
            if dx == 0 and dy == 0:
                acc = t
                continue
            if dy == 0:
                for x in xs:
                    s = place_of(x, 0)[0]
                    s_from = place_of(x - 8 * dx, 0)[0]
                    acc += jnp.where(group == s, roll(t, 8 * (s - s_from)), 0.0)
                singles = [(x, y) for (x, y) in singles if y in (-1, 8)]
            if dx == 0:
                row, s, s_from = (7, 10, 11) if dy == -1 else (0, 11, 10)
                rows = roll(skew(spread_row(t, row), -8), 8 * s)
                acc += jnp.where(group == s, rows, 0.0)
                rows = jnp.where(group == 0, roll(t, -8 * s_from), 0.0)
                rows = jnp.sum(skew(rows, 8), axis=0, keepdims=True)
                acc += jnp.where(sub == 7 - row, rows, 0.0)
                singles = [(x, y) for (x, y) in singles if x in (-1, 8)]
            for x, y in singles:
                s, r = place_of(x, y)
                s_from, r_from = place_of(x - 8 * dx, y - 8 * dy)
                got = spread_row(roll(t, 8 * (s - s_from)), r_from)
                acc += jnp.where((group == s) & (sub == r), got, 0.0)
        layers.append(acc)

    for s in range(13):
        for c in range(5):
            at = 8 * (5 * s + c)
            k = 8 * s + c
            v = dep[pl.ds(at, 8), :]
            v += jnp.where(lane == 0, roll(layers[0], -k), 0.0)
            v += jnp.where(lane == 127, roll(layers[1], 127 - k), 0.0)
            src[pl.ds(at, 8), :] = v
    def take(recv, singles, at):
        for n, (x, y) in enumerate(singles):
            s, r = place_of(x, y)
            src[pl.ds(40 * s + r, 5, stride=8), :] += recv[pl.ds(at + 8 * n, 5), :]

    near = {-1: (-1, 0), 1: (8, 7)}
    for n, sign in enumerate((-1, 1)):
        a, b = near[sign]
        for m, x in enumerate((a, b)):
            src[pl.ds(40 * place_of(x, 0)[0], 40), :] += x2recv[n, pl.ds(40 * m, 40), :]
        take(x2recv.at[n], [(a, -1), (a, 8), (b, -1), (b, 8)], 80)
        src[pl.ds(40 * place_of(0, a)[0], 40), :] += y2recv[n, pl.ds(0, 40), :]
        for c in range(5):
            src[pl.ds(8 * c + b, 8, stride=40), :] += y2recv[n, pl.ds(40 + 8 * c, 8), :]
        take(y2recv.at[n], [(-1, a), (8, a), (-1, b), (8, b)], 80)
    for j, (sx, sy) in enumerate(SIGNS):
        take(c2recv.at[j], [(x, y) for x in near[-sx] for y in near[-sy]], 0)

    def push_step(x, _):
        at = pl.multiple_of(x * 40, 8)
        to_row = pl.multiple_of(PITCH * (x + 1) + 8, 8)
        s = [src[pl.ds(at + 8 * c, 8), :] for c in range(5)]
        to[x] = gt[x] + s[3]
        vo[x] = gv[x] + s[4]
        for q in range(27):
            pop[q, pl.ds(to_row, 8), :] += push_of(q, s)
        return 0

    lax.fori_loop(0, 8, push_step, 0)
    s8, s9, s10, s11, s12 = (
        [src[pl.ds(8 * (5 * s + c), 8), :] for c in range(5)] for s in range(8, 13)
    )
    for k in range(9):
        pop[18 + k, pl.ds(8, 8), :] = xbrecv[0, k] + push_of(18 + k, s8)
        pop[k, pl.ds(PITCH * 9 + 8, 8), :] = xbrecv[1, k] + push_of(k, s9)
        q = Y_UP[k]
        pop[q, pl.ds(PITCH + 7, 8, stride=PITCH), :] = (
            ybrecv[0, pl.ds(8 * k, 8), :] + push_of(q, s10)
        )
        q = Y_DOWN[k]
        pop[q, pl.ds(PITCH + 16, 8, stride=PITCH), :] = (
            ybrecv[1, pl.ds(8 * k, 8), :] + push_of(q, s11)
        )
    for j, (sx, sy) in enumerate(SIGNS):
        row = PITCH * (0, 9)[j // 2] + (7, 16)[j % 2]
        for k in range(3):
            q = 9 * (sx + 1) + 3 * (sy + 1) + k
            total = crecv[j, pl.ds(5 + k, 1), :] + push_of(q, s12)[j : j + 1]
            pop[q, pl.ds(row, 1), :] = total

    number = lane - 5
    used = (number >= 0) & (number < 9)
    step_x = jnp.where(number < 3, -1.0, jnp.where(number < 6, 0.0, 1.0))
    third = jnp.where(number < 3, number, jnp.where(number < 6, number - 3, number - 6))
    step_y = jnp.where(third == 0, -1.0, jnp.where(third == 1, 0.0, 1.0))
    share = jnp.where(step_x == 0.0, 2.0 / 3.0, 1.0 / 6.0)
    share = share * jnp.where(step_y == 0.0, 2.0 / 3.0, 1.0 / 6.0)
    share = jnp.where(used, share * (1.0 / 6.0), 0.0)
    share_x = 3.0 * share * step_x
    share_y = 3.0 * share * step_y
    for side in range(2):
        for s in range(13):
            three = [
                jnp.broadcast_to(layers[side][:, 8 * s + v : 8 * s + v + 1], (8, 128))
                for v in (5, 6, 7)
            ]
            t = zslot[side, pl.ds(8 * s, 8), :]
            t = t + share * three[0] + share_x * three[1] + share_y * three[2]
            if s < 8:
                zcol[side, pl.ds(PITCH * (s + 1) + 8, 8), :] = t
            elif s < 10:
                zcol[side, pl.ds(PITCH * (0, 9)[s - 8] + 8, 8), :] = t
            elif s < 12:
                zcol[side, pl.ds(PITCH + (7, 16)[s - 10], 8, stride=PITCH), :] = t
            else:
                for j in range(4):
                    row = PITCH * (0, 9)[j // 2] + (7, 16)[j % 2]
                    zcol[side, pl.ds(row, 1), :] = t[j : j + 1]

    written = write([(to, to_out), (vo, vo_out), (mo, mo_out)], 0)
    for part in range(9):
        for q in range(3 * part, 3 * part + 3):
            ex, ey, ez = step_of(q)
            m = q // 3 + 5
            for x in range(8):
                row = PITCH * (x - ex + 1) + 8 - ey
                v = pop[q, pl.ds(row, 8), :]
                if ez == 1:
                    v = jnp.where(lane == 0, roll(zcol[0, pl.ds(row, 8), :], -m), roll(v, 1))
                elif ez == -1:
                    v = jnp.where(
                        lane == 127, roll(zcol[1, pl.ds(row, 8), :], 127 - m), roll(v, -1)
                    )
                staged[q, x] = v
        here = pl.ds(3 * part, 3)
        written += write([(staged.at[here], fo.at[here])], 3 + part)

    for copy in copies2:
        copy.wait_send()
    for copy in written:
        copy.wait()


def keep_kernel(a0, a1, a2, a3, b0, b1, b2, b3, t0, t1, t2, t3, sem):
    trips = []
    for part in range(3):
        here = pl.ds(9 * part, 9)
        trips.append((a0.at[here], t0.at[here], b0.at[here]))
    trips += [(a1, t1, b1), (a2, t2, b2), (a3, t3, b3)]
    copies = []
    for n, (a, t, _) in enumerate(trips):
        copy = pltpu.make_async_copy(a, t, sem.at[0, n])
        copy.start()
        copies.append(copy)
    outs = []
    for n, (_, t, b) in enumerate(trips):
        copies[n].wait()
        copy = pltpu.make_async_copy(t, b, sem.at[1, n])
        copy.start()
        outs.append(copy)
    for copy in outs:
        copy.wait()


def on_device(f, gt, gv, base, frac, vel, temp, rate, live):
    anywhere = pl.BlockSpec(memory_space=pl.ANY)

    def buffer(*shape, dtype=F32):
        return pltpu.VMEM(shape, dtype)

    results = (
        jax.ShapeDtypeStruct(f.shape, F32),
        jax.ShapeDtypeStruct(gt.shape, F32),
        jax.ShapeDtypeStruct(gv.shape, F32),
        jax.ShapeDtypeStruct((3, 1, PARCELS), F32),
    )
    inner = pl.pallas_call(
        gather_kernel,
        out_shape=results,
        in_specs=[anywhere] * 8 + [pl.BlockSpec(memory_space=pltpu.SMEM)],
        out_specs=[anywhere] * 4,
        scratch_shapes=[
            buffer(27, 10 * PITCH, 128),
            buffer(2, 10 * PITCH, 128),
            buffer(8, 8, 128),
            buffer(8, 8, 128),
            buffer(3, 1, PARCELS),
            buffer(27, 8, 8, 128),
            buffer(27, 8, 8, 128),
            buffer(8, 8, 128),
            buffer(8, 8, 128),
            buffer(3, 1, PARCELS, dtype=jnp.int32),
            buffer(3, 1, PARCELS),
            buffer(3, 1, PARCELS),
            buffer(1, PARCELS),
            buffer(1, PARCELS),
            buffer(528, 128),
            buffer(2, 40, 128),
            buffer(4, 8, 128),
            buffer(4, 8, 128),
            buffer(2, 8, 128),
            buffer(2, 9, 8, 128),
            buffer(2, 72, 128),
            buffer(2, 72, 128),
            buffer(2, 9, 8, 128),
            buffer(528, 384, dtype=BF16),
            buffer(384, PARCELS, dtype=BF16),
            buffer(256, PARCELS, dtype=BF16),
            buffer(128, PARCELS),
            buffer(8, PARCELS),
            buffer(8, PARCELS),
            buffer(8, PARCELS),
            buffer(8, PARCELS),
            buffer(528, 128),
            buffer(128, 128),
            buffer(2, 104, 128),
            buffer(128, 128),
            buffer(2, 120, 128),
            buffer(2, 120, 128),
            buffer(2, 120, 128),
            buffer(2, 120, 128),
            buffer(4, 40, 128),
            buffer(4, 40, 128),
            buffer(2, 8, 128),
            buffer(2, 9, 8, 128),
            buffer(528, 128),
            pltpu.SemaphoreType.DMA((8,)),
            pltpu.SemaphoreType.DMA((12,)),
            pltpu.SemaphoreType.DMA((2, 30)),
            pltpu.SemaphoreType.DMA((2, 30)),
        ],
        compiler_params=pltpu.CompilerParams(
            collective_id=0, has_side_effects=True, vmem_limit_bytes=56 * 1024 * 1024
        ),
    )(
        f,
        gt,
        gv,
        base.reshape(3, 1, PARCELS),
        frac.reshape(3, 1, PARCELS),
        vel.reshape(3, 1, PARCELS),
        temp.reshape(1, PARCELS),
        rate.reshape(1, PARCELS),
        live.reshape(1),
    )
    fo, to, vo, mo = pl.pallas_call(
        keep_kernel,
        out_shape=results,
        in_specs=[anywhere] * 4,
        out_specs=[anywhere] * 4,
        scratch_shapes=[
            buffer(*f.shape),
            buffer(*gt.shape),
            buffer(*gv.shape),
            buffer(3, 1, PARCELS),
            pltpu.SemaphoreType.DMA((2, 6)),
        ],
        compiler_params=pltpu.CompilerParams(vmem_limit_bytes=56 * 1024 * 1024),
    )(*inner)
    return fo, to, vo, mo.reshape(vel.shape)


def solution(mesh):
    placed = (
        P(None, "gx", "gy", "gz"),
        P("gx", "gy", "gz"),
        P("gx", "gy", "gz"),
        P(None, "gx", "gy", "gz", None),
        P(None, "gx", "gy", "gz", None),
        P(None, "gx", "gy", "gz", None),
        P("gx", "gy", "gz", None),
        P("gx", "gy", "gz", None),
        P("gx", "gy", "gz"),
    )
    return jax.shard_map(
        on_device,
        mesh=mesh,
        in_specs=placed,
        out_specs=(
            P(None, "gx", "gy", "gz"),
            P("gx", "gy", "gz"),
            P("gx", "gy", "gz"),
            P(None, "gx", "gy", "gz", None),
        ),
        check_vma=False,
    )
```

time: 45.8 us -> 35.1 us (0.77)
  local copies, waits for them, and re-layouts: 5.46 us -> 0 us
  Pallas kernels: 38.7 us -> 33.7 us
    unnamed x20 -> x0, local copies, waits for them, and re-layouts: 5.46 us -> none
    pallas_call x1 -> x2, Pallas kernels: 38.7 us -> 33.7 us  [the longest x1 31.7 us: on_device(): pl.pallas_call(gather_kernel, out_shape=results, in_specs=[anywhere] * 8...]
where the time goes in v2:
time: 35.1 us; the launch traced here: 34.9 us
  Pallas kernels  33.7 us (96%)
  between operations  1.29 us (4%)
    pallas_call x1, Pallas kernels, on_device(): pl.pallas_call(gather_kernel, out_shape=results, in_specs=[anywhere] * 8...  31.7 us
    pallas_call x1, Pallas kernels, on_device(): pl.pallas_call(keep_kernel, out_shape=results, in_specs=[anywhere] * 4, o...  1.99 us

profile of v2, /device:TPU:1, one launch (start us, length us, event | category | flops | bytes accessed | tf_op | source)
XLA Modules:
  0.0 34.9 jit_solution(16355975882245113878)
XLA Ops:
  1.3 31.7 %shard_map.120 = (f32[27,8,8,128]{3,2,1,0:T(8,128)}, f32[8,8,128]{2,1,0:T(8,128)}, f32[8,8,128]{2,1,0:T(8,128)}, f32[3,1,2048]{2,1,0:T(1,128)}) custom-call(f32[27,8,8,128]{3,2,1,0:T(8,128)} %f_in.1, f32[8,8,128]{2,1,0:T(8,128)} %gt_in.1, f32[8,8,128]{2,1,0:T(8,128)} %gv_in.1, s32[3,1,2048]{2,1,0:T(1,128)} %bitcast.10, f32[3,1,2048]{2,1,0:T(1,128)} %bitcast.11, ...), custom_call_target="tpu_custom_call" | custom-call | tf_op jit(solution)/shard_map/pallas_call | solution.py:663
  33.0 2.0 %shard_map.121 = (f32[27,8,8,128]{3,2,1,0:T(8,128)}, f32[8,8,128]{2,1,0:T(8,128)}, f32[8,8,128]{2,1,0:T(8,128)}, f32[3,1,2048]{2,1,0:T(1,128)}) custom-call(f32[27,8,8,128]{3,2,1,0:T(8,128)} %get-tuple-element.12.a0, f32[8,8,128]{2,1,0:T(8,128)} %get-tuple-element.13.a1, f32[8,8,128]{2,1,0:T(8,128)} %get-tuple-element.14.a2, f32[3,1,2048]{2,1,0:T(1,128)} %get-tuple-element.15.a3), custom_call_target="tpu_custom_call" | custom-call | tf_op jit(solution)/shard_map/pallas_call | solution.py:732

commit v3 on v2

--- a/solution.py
+++ b/solution.py
@@ -6,7 +6,7 @@
 from jax.sharding import PartitionSpec as P
 
 AXES = ("gx", "gy", "gz")
-CHUNK = 256
+CHUNK = 1024
 PARCELS = 2048
 PITCH = 24
 F32 = jnp.float32

time: 35.1 us -> 33.1 us (0.943)
  Pallas kernels: 33.7 us -> 31.6 us
    pallas_call x1, Pallas kernels: 31.7 us -> 29.7 us  [on_device(): pl.pallas_call(gather_kernel, out_shape=results, in_specs=[anywhere] * 8...]
where the time goes in v3:
time: 33.1 us; the launch traced here: 32.9 us
  Pallas kernels  31.6 us (95%)
  between operations  1.29 us (4%)
    pallas_call x1, Pallas kernels, on_device(): pl.pallas_call(gather_kernel, out_shape=results, in_specs=[anywhere] * 8...  29.7 us
    pallas_call x1, Pallas kernels, on_device(): pl.pallas_call(keep_kernel, out_shape=results, in_specs=[anywhere] * 4, o...  1.99 us

profile of v3, /device:TPU:1, one launch (start us, length us, event | category | flops | bytes accessed | tf_op | source)
XLA Modules:
  0.0 32.9 jit_solution(6268431977512422022)
XLA Ops:
  1.3 29.7 %shard_map.120 = (f32[27,8,8,128]{3,2,1,0:T(8,128)}, f32[8,8,128]{2,1,0:T(8,128)}, f32[8,8,128]{2,1,0:T(8,128)}, f32[3,1,2048]{2,1,0:T(1,128)}) custom-call(f32[27,8,8,128]{3,2,1,0:T(8,128)} %f_in.1, f32[8,8,128]{2,1,0:T(8,128)} %gt_in.1, f32[8,8,128]{2,1,0:T(8,128)} %gv_in.1, s32[3,1,2048]{2,1,0:T(1,128)} %bitcast.10, f32[3,1,2048]{2,1,0:T(1,128)} %bitcast.11, ...), custom_call_target="tpu_custom_call" | custom-call | tf_op jit(solution)/shard_map/pallas_call | solution.py:663
  30.9 2.0 %shard_map.121 = (f32[27,8,8,128]{3,2,1,0:T(8,128)}, f32[8,8,128]{2,1,0:T(8,128)}, f32[8,8,128]{2,1,0:T(8,128)}, f32[3,1,2048]{2,1,0:T(1,128)}) custom-call(f32[27,8,8,128]{3,2,1,0:T(8,128)} %get-tuple-element.12.a0, f32[8,8,128]{2,1,0:T(8,128)} %get-tuple-element.13.a1, f32[8,8,128]{2,1,0:T(8,128)} %get-tuple-element.14.a2, f32[3,1,2048]{2,1,0:T(1,128)} %get-tuple-element.15.a3), custom_call_target="tpu_custom_call" | custom-call | tf_op jit(solution)/shard_map/pallas_call | solution.py:732

commit v4 on v3

--- a/solution.py
+++ b/solution.py
@@ -114,9 +114,9 @@
             copies.append(copy)
         return copies
 
-    def exchange(phase, moves):
+    def exchange(phase, moves, at=0):
         copies = []
-        for n, (a, b, d) in enumerate(moves):
+        for n, (a, b, d) in enumerate(moves, start=at):
             copy = pltpu.make_async_remote_copy(
                 src_ref=a,
                 dst_ref=b,
@@ -237,6 +237,8 @@
         wmat[pl.ds(256, 128), here] = wz_hi
         edges[pl.ds(0, 1), here] = jnp.where(bz == -1, 1.0 - fz, 0.0)
         edges[pl.ds(1, 1), here] = jnp.where(bz == 127, fz, 0.0)
+        edges[pl.ds(2, 1), here] = jnp.where(bz == -1, fz, 0.0)
+        edges[pl.ds(3, 1), here] = jnp.where(bz == 127, 1.0 - fz, 0.0)
 
         wx8 = hat(rows8, bx, fx)
         wy8 = hat(rows8, by, fy)
@@ -293,18 +295,24 @@
 
     copies1 = exchange(
         0,
-        z_moves(zsend, zrecv)
-        + corner_moves(csend, crecv)
+        corner_moves(csend, crecv)
         + [
             (ysend.at[1], ext.at[pl.ds(400, 40)], (0, 1, 0)),
             (ysend.at[0], ext.at[pl.ds(440, 40)], (0, -1, 0)),
             (ext.at[pl.ds(280, 40)], ext.at[pl.ds(320, 40)], (1, 0, 0)),
             (ext.at[pl.ds(0, 40)], ext.at[pl.ds(360, 40)], (-1, 0, 0)),
+        ],
+    )
+    copies_z = exchange(0, z_moves(zsend, zrecv), 8)
+    copies_b = exchange(
+        0,
+        [
             (ybsend.at[1], ybrecv.at[0], (0, 1, 0)),
             (ybsend.at[0], ybrecv.at[1], (0, -1, 0)),
             (pop.at[pl.ds(18, 9), pl.ds(PITCH * 8 + 8, 8)], xbrecv.at[0], (1, 0, 0)),
             (pop.at[pl.ds(0, 9), pl.ds(PITCH + 8, 8)], xbrecv.at[1], (-1, 0, 0)),
         ],
+        26,
     )
 
     lax.fori_loop(0, 20, matrix_step, 0)
@@ -339,6 +347,43 @@
         ext[pl.ds(480 + 8 * c + 4, 4), :] = jnp.zeros((4, 128), F32)
     ext[pl.ds(520, 8), :] = zero8
 
+    lax.fori_loop(20, 33, matrix_step, 0)
+
+    def chunk_step(n, _):
+        here = pl.ds(pl.multiple_of(n * CHUNK, CHUNK), CHUNK)
+        below = edges[pl.ds(0, 1), here]
+        above = edges[pl.ds(1, 1), here]
+        along = jnp.dot(amat[pl.ds(320, 208), :], wmat[:, here], preferred_element_type=F32)
+        got = sampled[:, here] + sample(8, 13, along, here, 320)
+        terms = factor[:, here] * (target[:, here] - got)
+        for d in range(3):
+            mo[d, :, here] = target[pl.ds(d, 1), here] - 0.5 * terms[d : d + 1]
+
+        load = [
+            plane_of[pl.ds(8 * s, 8), here] * terms[c : c + 1] for s in range(13) for c in range(5)
+        ]
+        load.append(jnp.zeros((8, CHUNK), F32))
+        load_hi, load_lo = split(jnp.concatenate(load, axis=0))
+        got_hi = lax.dot_general(
+            load_hi, wmat[pl.ds(0, 256), here], NT, preferred_element_type=F32
+        )
+        got_lo = lax.dot_general(
+            load_lo, wmat[pl.ds(0, 128), here], NT, preferred_element_type=F32
+        )
+        dep[...] += got_hi[:, :128] + got_hi[:, 128:] + got_lo
+
+        side_hi, side_lo = split(jnp.concatenate([terms * below, terms * above], axis=0))
+        edge_hi = lax.dot_general(side_hi, pmat[:, here], NT, preferred_element_type=F32)
+        edge_lo = lax.dot_general(
+            side_lo, pmat[pl.ds(0, 128), here], NT, preferred_element_type=F32
+        )
+        rim[pl.ds(0, 16), :] += edge_hi[:, :128] + edge_hi[:, 128:] + edge_lo
+        return 0
+
+    lax.fori_loop(0, PARCELS // CHUNK, chunk_step, 0)
+
+    for copy in copies_z:
+        copy.wait_recv()
     rimf[pl.ds(104, 24), :] = jnp.zeros((24, 128), F32)
     for s in range(13):
         sides = []
@@ -371,50 +416,36 @@
         axis=0,
     )
 
-    lax.fori_loop(20, 33, matrix_step, 0)
-
-    def chunk_step(n, _):
+    def layer_step(n, _):
         here = pl.ds(pl.multiple_of(n * CHUNK, CHUNK), CHUNK)
-        below = edges[pl.ds(0, 1), here]
-        above = edges[pl.ds(1, 1), here]
-        along = jnp.dot(amat[pl.ds(320, 208), :], wmat[:, here], preferred_element_type=F32)
-        got = sampled[:, here] + sample(8, 13, along, here, 320)
+        below, above, first, last = (edges[pl.ds(k, 1), here] for k in range(4))
         ends = jnp.dot(rim_left, pmat[:, here], preferred_element_type=F32)
         ends = ends[:16] + ends[16:]
-        got = got + below * ends[:8] + above * ends[8:]
-        terms = factor[:, here] * (target[:, here] - got)
+        terms = -factor[:, here] * (below * ends[:8] + above * ends[8:])
         for d in range(3):
-            mo[d, :, here] = target[pl.ds(d, 1), here] - 0.5 * terms[d : d + 1]
-
-        load = [
-            plane_of[pl.ds(8 * s, 8), here] * terms[c : c + 1] for s in range(13) for c in range(5)
-        ]
-        load.append(jnp.zeros((8, CHUNK), F32))
-        load_hi, load_lo = split(jnp.concatenate(load, axis=0))
-        got_hi = lax.dot_general(
-            load_hi, wmat[pl.ds(0, 256), here], NT, preferred_element_type=F32
-        )
+            mo[d, :, here] -= 0.5 * terms[d : d + 1]
+        inside = [t[c : c + 1] for c in range(5) for t in (terms * last, terms * first)]
+        left = jnp.concatenate(
+            [terms * below, terms * above] + inside + [jnp.zeros((6, CHUNK), F32)], axis=0
+        )
+        left_hi, left_lo = split(left)
+        got_hi = lax.dot_general(left_hi, pmat[:, here], NT, preferred_element_type=F32)
         got_lo = lax.dot_general(
-            load_lo, wmat[pl.ds(0, 128), here], NT, preferred_element_type=F32
-        )
-        dep[...] += got_hi[:, :128] + got_hi[:, 128:] + got_lo
-
-        side_hi, side_lo = split(jnp.concatenate([terms * below, terms * above], axis=0))
-        edge_hi = lax.dot_general(side_hi, pmat[:, here], NT, preferred_element_type=F32)
-        edge_lo = lax.dot_general(
-            side_lo, pmat[pl.ds(0, 128), here], NT, preferred_element_type=F32
-        )
-        rim[pl.ds(0, 16), :] += edge_hi[:, :128] + edge_hi[:, 128:] + edge_lo
+            left_lo, pmat[pl.ds(0, 128), here], NT, preferred_element_type=F32
+        )
+        rim[pl.ds(0, 32), :] += got_hi[:, :128] + got_hi[:, 128:] + got_lo
         return 0
 
-    lax.fori_loop(0, PARCELS // CHUNK, chunk_step, 0)
+    lax.fori_loop(0, PARCELS // CHUNK, layer_step, 0)
 
     by_row = jnp.transpose(rim[...])
+    outer = (lane == 0) | (lane == 127)
     low = zero8
     high = zero8
     for s in range(13):
         v = by_row[8 * s : 8 * s + 8]
-        own = [dep[pl.ds(8 * (5 * s + c), 8), :] for c in range(5)]
+        for c in range(5):
+            dep[pl.ds(8 * (5 * s + c), 8), :] += jnp.where(outer, roll(v, -17 - 2 * c), 0.0)
         mine = group == s
         low = jnp.where(mine, roll(v, 8 * s), low)
         high = jnp.where(mine, roll(v, 8 * s - 8), high)
@@ -472,8 +503,10 @@
             (x2send.at[0], x2recv.at[1], (-1, 0, 0)),
         ],
     )
-    for copy in copies1:
+    for copy in copies1 + copies_z + copies_b:
         copy.wait_send()
+    for copy in copies_b:
+        copy.wait_recv()
     for copy in copies2:
         copy.wait_recv()
 

time: 33.1 us -> 32 us (0.967)
  Pallas kernels: 31.6 us -> 30.5 us
    pallas_call x1, Pallas kernels: 29.7 us -> 28.5 us  [on_device(): pl.pallas_call(gather_kernel, out_shape=results, in_specs=[anywhere] * 8...]
where the time goes in v4:
time: 32 us; the launch traced here: 31.8 us
  Pallas kernels  30.5 us (95%)
  between operations  1.29 us (4%)
    pallas_call x1, Pallas kernels, on_device(): pl.pallas_call(gather_kernel, out_shape=results, in_specs=[anywhere] * 8...  28.5 us
    pallas_call x1, Pallas kernels, on_device(): pl.pallas_call(keep_kernel, out_shape=results, in_specs=[anywhere] * 4, o...  1.99 us

profile of v4, /device:TPU:1, one launch (start us, length us, event | category | flops | bytes accessed | tf_op | source)
XLA Modules:
  0.0 31.8 jit_solution(6647838409797703862)
XLA Ops:
  1.3 28.5 %shard_map.120 = (f32[27,8,8,128]{3,2,1,0:T(8,128)}, f32[8,8,128]{2,1,0:T(8,128)}, f32[8,8,128]{2,1,0:T(8,128)}, f32[3,1,2048]{2,1,0:T(1,128)}) custom-call(f32[27,8,8,128]{3,2,1,0:T(8,128)} %f_in.1, f32[8,8,128]{2,1,0:T(8,128)} %gt_in.1, f32[8,8,128]{2,1,0:T(8,128)} %gv_in.1, s32[3,1,2048]{2,1,0:T(1,128)} %bitcast.10, f32[3,1,2048]{2,1,0:T(1,128)} %bitcast.11, ...), custom_call_target="tpu_custom_call" | custom-call | tf_op jit(solution)/shard_map/pallas_call | solution.py:696
  29.8 2.0 %shard_map.121 = (f32[27,8,8,128]{3,2,1,0:T(8,128)}, f32[8,8,128]{2,1,0:T(8,128)}, f32[8,8,128]{2,1,0:T(8,128)}, f32[3,1,2048]{2,1,0:T(1,128)}) custom-call(f32[27,8,8,128]{3,2,1,0:T(8,128)} %get-tuple-element.12.a0, f32[8,8,128]{2,1,0:T(8,128)} %get-tuple-element.13.a1, f32[8,8,128]{2,1,0:T(8,128)} %get-tuple-element.14.a2, f32[3,1,2048]{2,1,0:T(1,128)} %get-tuple-element.15.a3), custom_call_target="tpu_custom_call" | custom-call | tf_op jit(solution)/shard_map/pallas_call | solution.py:765

commit v5 on v4

--- a/solution.py
+++ b/solution.py
@@ -71,7 +71,7 @@
     pop, zcol, to, vo, mo, staged,
     f, gt, gv, base, frac, vel, temp, rate,
     ext, ysend, csend, crecv, zsend, zrecv, ybsend, ybrecv, xbrecv,
-    amat, wmat, pmat, plane_of, target, factor, sampled, edges,
+    amat, wmat, pmat, plane_of, target, factor, sampled, edges, terms_of, left,
     dep, rim, zslot, rimf,
     x2send, x2recv, y2send, y2recv, c2send, c2recv, z2send, z2recv, src,
     in_sem, out_sem, send_sem, recv_sem,
@@ -237,8 +237,8 @@
         wmat[pl.ds(256, 128), here] = wz_hi
         edges[pl.ds(0, 1), here] = jnp.where(bz == -1, 1.0 - fz, 0.0)
         edges[pl.ds(1, 1), here] = jnp.where(bz == 127, fz, 0.0)
-        edges[pl.ds(2, 1), here] = jnp.where(bz == -1, fz, 0.0)
-        edges[pl.ds(3, 1), here] = jnp.where(bz == 127, 1.0 - fz, 0.0)
+        edges[pl.ds(2, 1), here] = hat(0, bz, fz)
+        edges[pl.ds(3, 1), here] = hat(127, bz, fz)
 
         wx8 = hat(rows8, bx, fx)
         wy8 = hat(rows8, by, fy)
@@ -337,6 +337,7 @@
     lax.fori_loop(0, PARCELS // CHUNK, own_step, 0)
     dep[...] = jnp.zeros_like(dep)
     rim[...] = jnp.zeros_like(rim)
+    left[...] = jnp.zeros_like(left)
 
     for copy in copies1:
         copy.wait_recv()
@@ -349,16 +350,16 @@
 
     lax.fori_loop(20, 33, matrix_step, 0)
 
-    def chunk_step(n, _):
+    def term_step(n, _):
         here = pl.ds(pl.multiple_of(n * CHUNK, CHUNK), CHUNK)
-        below = edges[pl.ds(0, 1), here]
-        above = edges[pl.ds(1, 1), here]
         along = jnp.dot(amat[pl.ds(320, 208), :], wmat[:, here], preferred_element_type=F32)
         got = sampled[:, here] + sample(8, 13, along, here, 320)
-        terms = factor[:, here] * (target[:, here] - got)
-        for d in range(3):
-            mo[d, :, here] = target[pl.ds(d, 1), here] - 0.5 * terms[d : d + 1]
-
+        terms_of[:, here] = factor[:, here] * (target[:, here] - got)
+        return 0
+
+    def load_step(n, _):
+        here = pl.ds(pl.multiple_of(n * CHUNK, CHUNK), CHUNK)
+        terms = terms_of[:, here]
         load = [
             plane_of[pl.ds(8 * s, 8), here] * terms[c : c + 1] for s in range(13) for c in range(5)
         ]
@@ -371,16 +372,10 @@
             load_lo, wmat[pl.ds(0, 128), here], NT, preferred_element_type=F32
         )
         dep[...] += got_hi[:, :128] + got_hi[:, 128:] + got_lo
-
-        side_hi, side_lo = split(jnp.concatenate([terms * below, terms * above], axis=0))
-        edge_hi = lax.dot_general(side_hi, pmat[:, here], NT, preferred_element_type=F32)
-        edge_lo = lax.dot_general(
-            side_lo, pmat[pl.ds(0, 128), here], NT, preferred_element_type=F32
-        )
-        rim[pl.ds(0, 16), :] += edge_hi[:, :128] + edge_hi[:, 128:] + edge_lo
         return 0
 
-    lax.fori_loop(0, PARCELS // CHUNK, chunk_step, 0)
+    lax.fori_loop(0, PARCELS // CHUNK, term_step, 0)
+    lax.fori_loop(0, PARCELS // CHUNK // 2, load_step, 0)
 
     for copy in copies_z:
         copy.wait_recv()
@@ -421,52 +416,52 @@
         below, above, first, last = (edges[pl.ds(k, 1), here] for k in range(4))
         ends = jnp.dot(rim_left, pmat[:, here], preferred_element_type=F32)
         ends = ends[:16] + ends[16:]
-        terms = -factor[:, here] * (below * ends[:8] + above * ends[8:])
+        terms = terms_of[:, here] - factor[:, here] * (below * ends[:8] + above * ends[8:])
         for d in range(3):
-            mo[d, :, here] -= 0.5 * terms[d : d + 1]
-        inside = [t[c : c + 1] for c in range(5) for t in (terms * last, terms * first)]
-        left = jnp.concatenate(
-            [terms * below, terms * above] + inside + [jnp.zeros((6, CHUNK), F32)], axis=0
-        )
-        left_hi, left_lo = split(left)
+            mo[d, :, here] = target[pl.ds(d, 1), here] - 0.5 * terms[d : d + 1]
+        t = [terms[c : c + 1] for c in range(5)]
+        lean = 3.0 * t[2]
+        up = [t[4] + lean, t[0], t[1]]
+        down = [t[4] - lean, t[0], t[1]]
+        rows = [v * below for v in t] + [v * first for v in down]
+        rows += [v * above for v in t] + [v * last for v in up]
+        rows += [v * below for v in up] + [None] + [v * above for v in down] + [None]
+        rows += [v * w for v in t for w in (last, first)]
+        for k, row in enumerate(rows):
+            if row is not None:
+                left[pl.ds(k, 1), here] = row
+        left_hi, left_lo = split(left[:, here])
         got_hi = lax.dot_general(left_hi, pmat[:, here], NT, preferred_element_type=F32)
         got_lo = lax.dot_general(
             left_lo, pmat[pl.ds(0, 128), here], NT, preferred_element_type=F32
         )
-        rim[pl.ds(0, 32), :] += got_hi[:, :128] + got_hi[:, 128:] + got_lo
+        rim[pl.ds(0, 48), :] += got_hi[:, :128] + got_hi[:, 128:] + got_lo
         return 0
 
     lax.fori_loop(0, PARCELS // CHUNK, layer_step, 0)
 
-    by_row = jnp.transpose(rim[...])
-    outer = (lane == 0) | (lane == 127)
+    rimf[...] = jnp.transpose(rim[...])
     low = zero8
     high = zero8
+    ring = zero8
     for s in range(13):
-        v = by_row[8 * s : 8 * s + 8]
-        for c in range(5):
-            dep[pl.ds(8 * (5 * s + c), 8), :] += jnp.where(outer, roll(v, -17 - 2 * c), 0.0)
+        v = rimf[pl.ds(8 * s, 8), :]
         mine = group == s
         low = jnp.where(mine, roll(v, 8 * s), low)
         high = jnp.where(mine, roll(v, 8 * s - 8), high)
-    ring = jnp.where(
-        low_lane == 0,
-        roll(low, -4) + 3.0 * roll(low, -2),
-        jnp.where(
-            low_lane < 3,
-            roll(low, 1),
-            jnp.where(low_lane == 4, high - 3.0 * roll(high, 2), roll(high, 5)),
-        ),
-    )
-    for s in range(13):
-        own = [dep[pl.ds(8 * (5 * s + c), 8), :] for c in range(5)]
-        lean = 3.0 * own[2]
-        for v, (a, b) in enumerate([(own[4] - lean, own[4] + lean), (own[0],) * 2, (own[1],) * 2]):
-            at = 8 * s + 5 + v
-            low = jnp.where(lane == at, roll(a, at), low)
-            high = jnp.where(lane == at, roll(b, at + 1), high)
+        ring = jnp.where(mine, roll(v, 8 * s - 16), ring)
     z2send[0] = low
     z2send[1] = high
+    copies2 = exchange(1, z_moves(z2send, z2recv))
+
+    lax.fori_loop(PARCELS // CHUNK // 2, PARCELS // CHUNK, load_step, 0)
+
+    outer = (lane == 0) | (lane == 127)
+    for s in range(13):
+        v = rimf[pl.ds(8 * s, 8), :]
+        for c in range(5):
+            here = pl.ds(8 * (5 * s + c), 8)
+            dep[here, :] = jnp.where(outer, roll(v, -25 - 2 * c), dep[here, :])
 
     def fill(send, blocks, singles, at):
         for n, block in enumerate(blocks):
@@ -492,16 +487,16 @@
     for j, (sx, sy) in enumerate(SIGNS):
         fill(c2send.at[j], [], [(x, y) for x in far[sx] for y in far[sy]], 0)
 
-    copies2 = exchange(
+    copies2 += exchange(
         1,
-        z_moves(z2send, z2recv)
-        + corner_moves(c2send, c2recv)
+        corner_moves(c2send, c2recv)
         + [
             (y2send.at[1], y2recv.at[0], (0, 1, 0)),
             (y2send.at[0], y2recv.at[1], (0, -1, 0)),
             (x2send.at[1], x2recv.at[0], (1, 0, 0)),
             (x2send.at[0], x2recv.at[1], (-1, 0, 0)),
         ],
+        18,
     )
     for copy in copies1 + copies_z + copies_b:
         copy.wait_send()
@@ -730,6 +725,8 @@
             buffer(8, PARCELS),
             buffer(8, PARCELS),
             buffer(8, PARCELS),
+            buffer(8, PARCELS),
+            buffer(48, PARCELS),
             buffer(528, 128),
             buffer(128, 128),
             buffer(2, 104, 128),

time: 32 us -> 31.9 us (level)
  no operation moved by 1% of the time
where the time goes in v5:
time: 31.9 us; the launch traced here: 31.7 us
  Pallas kernels  30.4 us (95%)
  between operations  1.29 us (4%)
    pallas_call x1, Pallas kernels, on_device(): pl.pallas_call(gather_kernel, out_shape=results, in_specs=[anywhere] * 8...  28.4 us
    pallas_call x1, Pallas kernels, on_device(): pl.pallas_call(keep_kernel, out_shape=results, in_specs=[anywhere] * 4, o...  1.99 us

profile of v5, /device:TPU:1, one launch (start us, length us, event | category | flops | bytes accessed | tf_op | source)
XLA Modules:
  0.0 31.7 jit_solution(7768663468522708948)
XLA Ops:
  1.3 28.4 %shard_map.120 = (f32[27,8,8,128]{3,2,1,0:T(8,128)}, f32[8,8,128]{2,1,0:T(8,128)}, f32[8,8,128]{2,1,0:T(8,128)}, f32[3,1,2048]{2,1,0:T(1,128)}) custom-call(f32[27,8,8,128]{3,2,1,0:T(8,128)} %f_in.1, f32[8,8,128]{2,1,0:T(8,128)} %gt_in.1, f32[8,8,128]{2,1,0:T(8,128)} %gv_in.1, s32[3,1,2048]{2,1,0:T(1,128)} %bitcast.10, f32[3,1,2048]{2,1,0:T(1,128)} %bitcast.11, ...), custom_call_target="tpu_custom_call" | custom-call | tf_op jit(solution)/shard_map/pallas_call | solution.py:691
  29.7 2.0 %shard_map.121 = (f32[27,8,8,128]{3,2,1,0:T(8,128)}, f32[8,8,128]{2,1,0:T(8,128)}, f32[8,8,128]{2,1,0:T(8,128)}, f32[3,1,2048]{2,1,0:T(1,128)}) custom-call(f32[27,8,8,128]{3,2,1,0:T(8,128)} %get-tuple-element.12.a0, f32[8,8,128]{2,1,0:T(8,128)} %get-tuple-element.13.a1, f32[8,8,128]{2,1,0:T(8,128)} %get-tuple-element.14.a2, f32[3,1,2048]{2,1,0:T(1,128)} %get-tuple-element.15.a3), custom_call_target="tpu_custom_call" | custom-call | tf_op jit(solution)/shard_map/pallas_call | solution.py:762

commit v6 on v5

--- a/solution.py
+++ b/solution.py
@@ -6,7 +6,8 @@
 from jax.sharding import PartitionSpec as P
 
 AXES = ("gx", "gy", "gz")
-CHUNK = 1024
+CHUNK = 2048
+LOAD = 1024
 PARCELS = 2048
 PITCH = 24
 F32 = jnp.float32
@@ -73,7 +74,7 @@
     ext, ysend, csend, crecv, zsend, zrecv, ybsend, ybrecv, xbrecv,
     amat, wmat, pmat, plane_of, target, factor, sampled, edges, terms_of, left,
     dep, rim, zslot, rimf,
-    x2send, x2recv, y2send, y2recv, c2send, c2recv, z2send, z2recv, src,
+    x2send, x2recv, y2send, y2recv, c2send, c2recv, z2send, z2recv, zsum, src,
     in_sem, out_sem, send_sem, recv_sem,
 ):
     me = [lax.axis_index(a) for a in AXES]
@@ -91,6 +92,7 @@
         for dy in (-1, 1, 0)
         if (dx, dy, dz) != (0, 0, 0)
     ]
+    around.sort(key=lambda d: -sum(map(abs, d)))
     barrier = pltpu.get_barrier_semaphore()
     for d in around:
         pl.semaphore_signal(barrier, inc=1, device_id=device(d), device_id_type=MESH)
@@ -267,7 +269,6 @@
         factor[:, here] = jnp.where(slot < alive, rate[:, here], 0.0) * scale
         return 0
 
-    lax.fori_loop(0, PARCELS // CHUNK, weight_step, 0)
 
     def matrix_step(n, _):
         at = pl.multiple_of(n * 16, 16)
@@ -315,6 +316,7 @@
         26,
     )
 
+    lax.fori_loop(0, PARCELS // CHUNK, weight_step, 0)
     lax.fori_loop(0, 20, matrix_step, 0)
 
     def sample(first_slot, last_slot, along, here, off):
@@ -358,12 +360,12 @@
         return 0
 
     def load_step(n, _):
-        here = pl.ds(pl.multiple_of(n * CHUNK, CHUNK), CHUNK)
+        here = pl.ds(pl.multiple_of(n * LOAD, LOAD), LOAD)
         terms = terms_of[:, here]
         load = [
             plane_of[pl.ds(8 * s, 8), here] * terms[c : c + 1] for s in range(13) for c in range(5)
         ]
-        load.append(jnp.zeros((8, CHUNK), F32))
+        load.append(jnp.zeros((8, LOAD), F32))
         load_hi, load_lo = split(jnp.concatenate(load, axis=0))
         got_hi = lax.dot_general(
             load_hi, wmat[pl.ds(0, 256), here], NT, preferred_element_type=F32
@@ -375,7 +377,7 @@
         return 0
 
     lax.fori_loop(0, PARCELS // CHUNK, term_step, 0)
-    lax.fori_loop(0, PARCELS // CHUNK // 2, load_step, 0)
+    lax.fori_loop(0, PARCELS // LOAD // 2, load_step, 0)
 
     for copy in copies_z:
         copy.wait_recv()
@@ -419,28 +421,27 @@
         terms = terms_of[:, here] - factor[:, here] * (below * ends[:8] + above * ends[8:])
         for d in range(3):
             mo[d, :, here] = target[pl.ds(d, 1), here] - 0.5 * terms[d : d + 1]
-        t = [terms[c : c + 1] for c in range(5)]
-        lean = 3.0 * t[2]
-        up = [t[4] + lean, t[0], t[1]]
-        down = [t[4] - lean, t[0], t[1]]
-        rows = [v * below for v in t] + [v * first for v in down]
-        rows += [v * above for v in t] + [v * last for v in up]
-        rows += [v * below for v in up] + [None] + [v * above for v in down] + [None]
-        rows += [v * w for v in t for w in (last, first)]
-        for k, row in enumerate(rows):
-            if row is not None:
-                left[pl.ds(k, 1), here] = row
-        left_hi, left_lo = split(left[:, here])
+        left_hi, left_lo = split(
+            jnp.concatenate([terms * w for w in (below, above, first, last)], axis=0)
+        )
         got_hi = lax.dot_general(left_hi, pmat[:, here], NT, preferred_element_type=F32)
         got_lo = lax.dot_general(
             left_lo, pmat[pl.ds(0, 128), here], NT, preferred_element_type=F32
         )
-        rim[pl.ds(0, 48), :] += got_hi[:, :128] + got_hi[:, 128:] + got_lo
+        rim[pl.ds(0, 32), :] += got_hi[:, :128] + got_hi[:, 128:] + got_lo
         return 0
 
     lax.fori_loop(0, PARCELS // CHUNK, layer_step, 0)
 
-    rimf[...] = jnp.transpose(rim[...])
+    layer = [[rim[pl.ds(8 * k + c, 1), :] for c in range(5)] for k in range(4)]
+    up = [[t[4] + 3.0 * t[2], t[0], t[1]] for t in layer]
+    down = [[t[4] - 3.0 * t[2], t[0], t[1]] for t in layer]
+    rows = layer[0] + down[2] + layer[1] + up[3] + up[0] + [None] + down[1] + [None]
+    rows += [t for c in range(5) for t in (layer[3][c], layer[2][c])]
+    for k, row in enumerate(rows):
+        if row is not None:
+            left[pl.ds(k, 1), :] = row
+    rimf[...] = jnp.transpose(left[...])
     low = zero8
     high = zero8
     ring = zero8
@@ -454,7 +455,7 @@
     z2send[1] = high
     copies2 = exchange(1, z_moves(z2send, z2recv))
 
-    lax.fori_loop(PARCELS // CHUNK // 2, PARCELS // CHUNK, load_step, 0)
+    lax.fori_loop(PARCELS // LOAD // 2, PARCELS // LOAD, load_step, 0)
 
     outer = (lane == 0) | (lane == 127)
     for s in range(13):
@@ -511,37 +512,49 @@
         rings[0, sign] = y2recv[n, pl.ds(112, 8), :]
     for j, (sx, sy) in enumerate(SIGNS):
         rings[-sx, -sy] = c2recv[j, pl.ds(32, 8), :]
+    for (dx, dy), ring_at in rings.items():
+        n = side_index(dx, dy)
+        for side in range(2):
+            zsum[side, n] = z2recv[side, n] + jnp.where(
+                low_lane >= 5, roll(ring_at, (5, 1)[side]), 0.0
+            )
     layers = []
     for side in range(2):
-        acc = None
-        for (dx, dy), ring_at in rings.items():
-            t = z2recv[side, side_index(dx, dy)]
-            t += jnp.where(low_lane >= 5, roll(ring_at, (5, 1)[side]), 0.0)
+        acc = zsum[side, side_index(0, 0)]
+        by_shift = {}
+
+        def move(shift, mask, v):
+            v = jnp.where(mask, v, 0.0)
+            by_shift[shift] = by_shift[shift] + v if shift in by_shift else v
+
+        for dx, dy in rings:
+            if dx == 0 and dy == 0:
+                continue
+            n = side_index(dx, dy)
             xs = {0: range(-1, 9), -1: (-1, 0), 1: (7, 8)}[dx]
             ys = {0: range(-1, 9), -1: (-1, 0), 1: (7, 8)}[dy]
             singles = [(x, y) for x in xs for y in ys]
-            if dx == 0 and dy == 0:
-                acc = t
-                continue
             if dy == 0:
                 for x in xs:
                     s = place_of(x, 0)[0]
                     s_from = place_of(x - 8 * dx, 0)[0]
-                    acc += jnp.where(group == s, roll(t, 8 * (s - s_from)), 0.0)
+                    move(s - s_from, group == s_from, zsum[side, n])
                 singles = [(x, y) for (x, y) in singles if y in (-1, 8)]
             if dx == 0:
                 row, s, s_from = (7, 10, 11) if dy == -1 else (0, 11, 10)
-                rows = roll(skew(spread_row(t, row), -8), 8 * s)
-                acc += jnp.where(group == s, rows, 0.0)
-                rows = jnp.where(group == 0, roll(t, -8 * s_from), 0.0)
+                line = jnp.broadcast_to(zsum[side, n, pl.ds(row, 1), :], (8, 128))
+                move(s, group == 0, skew(line, -8))
+                rows = jnp.where(group == 0, roll(zsum[side, n], -8 * s_from), 0.0)
                 rows = jnp.sum(skew(rows, 8), axis=0, keepdims=True)
                 acc += jnp.where(sub == 7 - row, rows, 0.0)
                 singles = [(x, y) for (x, y) in singles if x in (-1, 8)]
             for x, y in singles:
                 s, r = place_of(x, y)
                 s_from, r_from = place_of(x - 8 * dx, y - 8 * dy)
-                got = spread_row(roll(t, 8 * (s - s_from)), r_from)
-                acc += jnp.where((group == s) & (sub == r), got, 0.0)
+                line = jnp.broadcast_to(zsum[side, n, pl.ds(r_from, 1), :], (8, 128))
+                move(s - s_from, (group == s_from) & (sub == r), line)
+        for shift, v in by_shift.items():
+            acc += roll(v, 8 * shift)
         layers.append(acc)
 
     for s in range(13):
@@ -726,7 +739,7 @@
             buffer(8, PARCELS),
             buffer(8, PARCELS),
             buffer(8, PARCELS),
-            buffer(48, PARCELS),
+            buffer(128, 128),
             buffer(528, 128),
             buffer(128, 128),
             buffer(2, 104, 128),
@@ -738,6 +751,7 @@
             buffer(4, 40, 128),
             buffer(4, 40, 128),
             buffer(2, 8, 128),
+            buffer(2, 9, 8, 128),
             buffer(2, 9, 8, 128),
             buffer(528, 128),
             pltpu.SemaphoreType.DMA((8,)),

time: 31.9 us -> 31.1 us (0.975)
  Pallas kernels: 30.4 us -> 29.7 us
    pallas_call x1, Pallas kernels: 28.4 us -> 27.7 us  [on_device(): pl.pallas_call(gather_kernel, out_shape=results, in_specs=[anywhere] * 8...]
where the time goes in v6:
time: 31.1 us; the launch traced here: 31 us
  Pallas kernels  29.7 us (95%)
  between operations  1.29 us (4%)
    pallas_call x1, Pallas kernels, on_device(): pl.pallas_call(gather_kernel, out_shape=results, in_specs=[anywhere] * 8...  27.7 us
    pallas_call x1, Pallas kernels, on_device(): pl.pallas_call(keep_kernel, out_shape=results, in_specs=[anywhere] * 4, o...  1.99 us

profile of v6, /device:TPU:1, one launch (start us, length us, event | category | flops | bytes accessed | tf_op | source)
XLA Modules:
  0.0 31.0 jit_solution(4519235849492715122)
XLA Ops:
  1.3 27.7 %shard_map.120 = (f32[27,8,8,128]{3,2,1,0:T(8,128)}, f32[8,8,128]{2,1,0:T(8,128)}, f32[8,8,128]{2,1,0:T(8,128)}, f32[3,1,2048]{2,1,0:T(1,128)}) custom-call(f32[27,8,8,128]{3,2,1,0:T(8,128)} %f_in.1, f32[8,8,128]{2,1,0:T(8,128)} %gt_in.1, f32[8,8,128]{2,1,0:T(8,128)} %gv_in.1, s32[3,1,2048]{2,1,0:T(1,128)} %bitcast.10, f32[3,1,2048]{2,1,0:T(1,128)} %bitcast.11, ...), custom_call_target="tpu_custom_call" | custom-call | tf_op jit(solution)/shard_map/pallas_call | solution.py:704
  29.0 2.0 %shard_map.121 = (f32[27,8,8,128]{3,2,1,0:T(8,128)}, f32[8,8,128]{2,1,0:T(8,128)}, f32[8,8,128]{2,1,0:T(8,128)}, f32[3,1,2048]{2,1,0:T(1,128)}) custom-call(f32[27,8,8,128]{3,2,1,0:T(8,128)} %get-tuple-element.12.a0, f32[8,8,128]{2,1,0:T(8,128)} %get-tuple-element.13.a1, f32[8,8,128]{2,1,0:T(8,128)} %get-tuple-element.14.a2, f32[3,1,2048]{2,1,0:T(1,128)} %get-tuple-element.15.a3), custom_call_target="tpu_custom_call" | custom-call | tf_op jit(solution)/shard_map/pallas_call | solution.py:776

commit v7 on v6

--- a/solution.py
+++ b/solution.py
@@ -615,6 +615,26 @@
             total = crecv[j, pl.ds(5 + k, 1), :] + push_of(q, s12)[j : j + 1]
             pop[q, pl.ds(row, 1), :] = total
 
+    written = write([(to, to_out), (vo, vo_out), (mo, mo_out)], 0)
+
+    def run(ez):
+        for m in range(9):
+            q = 3 * m + 1 + ez
+            ex, ey, _ = step_of(q)
+            for x in range(8):
+                row = PITCH * (x - ex + 1) + 8 - ey
+                v = pop[q, pl.ds(row, 8), :]
+                if ez == 1:
+                    end = roll(zcol[0, pl.ds(row, 8), :], -m - 5)
+                    v = jnp.where(lane == 0, end, roll(v, 1))
+                elif ez == -1:
+                    end = roll(zcol[1, pl.ds(row, 8), :], 122 - m)
+                    v = jnp.where(lane == 127, end, roll(v, -1))
+                staged[q, x] = v
+            written.extend(write([(staged.at[q], fo.at[q])], 3 + q))
+
+    run(0)
+
     number = lane - 5
     used = (number >= 0) & (number < 9)
     step_x = jnp.where(number < 3, -1.0, jnp.where(number < 6, 0.0, 1.0))
@@ -644,23 +664,8 @@
                     row = PITCH * (0, 9)[j // 2] + (7, 16)[j % 2]
                     zcol[side, pl.ds(row, 1), :] = t[j : j + 1]
 
-    written = write([(to, to_out), (vo, vo_out), (mo, mo_out)], 0)
-    for part in range(9):
-        for q in range(3 * part, 3 * part + 3):
-            ex, ey, ez = step_of(q)
-            m = q // 3 + 5
-            for x in range(8):
-                row = PITCH * (x - ex + 1) + 8 - ey
-                v = pop[q, pl.ds(row, 8), :]
-                if ez == 1:
-                    v = jnp.where(lane == 0, roll(zcol[0, pl.ds(row, 8), :], -m), roll(v, 1))
-                elif ez == -1:
-                    v = jnp.where(
-                        lane == 127, roll(zcol[1, pl.ds(row, 8), :], 127 - m), roll(v, -1)
-                    )
-                staged[q, x] = v
-        here = pl.ds(3 * part, 3)
-        written += write([(staged.at[here], fo.at[here])], 3 + part)
+    run(1)
+    run(-1)
 
     for copy in copies2:
         copy.wait_send()
@@ -755,7 +760,7 @@
             buffer(2, 9, 8, 128),
             buffer(528, 128),
             pltpu.SemaphoreType.DMA((8,)),
-            pltpu.SemaphoreType.DMA((12,)),
+            pltpu.SemaphoreType.DMA((30,)),
             pltpu.SemaphoreType.DMA((2, 30)),
             pltpu.SemaphoreType.DMA((2, 30)),
         ],

time: 31.1 us -> 31.2 us (level)
  no operation moved by 1% of the time
where the time goes in v7:
time: 31.2 us; the launch traced here: 31.1 us
  Pallas kernels  29.8 us (96%)
  between operations  1.29 us (4%)
    pallas_call x1, Pallas kernels, on_device(): pl.pallas_call(gather_kernel, out_shape=results, in_specs=[anywhere] * 8...  27.8 us
    pallas_call x1, Pallas kernels, on_device(): pl.pallas_call(keep_kernel, out_shape=results, in_specs=[anywhere] * 4, o...  1.99 us

profile of v7, /device:TPU:1, one launch (start us, length us, event | category | flops | bytes accessed | tf_op | source)
XLA Modules:
  0.0 31.1 jit_solution(9676730144521115873)
XLA Ops:
  1.3 27.8 %shard_map.120 = (f32[27,8,8,128]{3,2,1,0:T(8,128)}, f32[8,8,128]{2,1,0:T(8,128)}, f32[8,8,128]{2,1,0:T(8,128)}, f32[3,1,2048]{2,1,0:T(1,128)}) custom-call(f32[27,8,8,128]{3,2,1,0:T(8,128)} %f_in.1, f32[8,8,128]{2,1,0:T(8,128)} %gt_in.1, f32[8,8,128]{2,1,0:T(8,128)} %gv_in.1, s32[3,1,2048]{2,1,0:T(1,128)} %bitcast.10, f32[3,1,2048]{2,1,0:T(1,128)} %bitcast.11, ...), custom_call_target="tpu_custom_call" | custom-call | tf_op jit(solution)/shard_map/pallas_call | solution.py:709
  29.1 2.0 %shard_map.121 = (f32[27,8,8,128]{3,2,1,0:T(8,128)}, f32[8,8,128]{2,1,0:T(8,128)}, f32[8,8,128]{2,1,0:T(8,128)}, f32[3,1,2048]{2,1,0:T(1,128)}) custom-call(f32[27,8,8,128]{3,2,1,0:T(8,128)} %get-tuple-element.12.a0, f32[8,8,128]{2,1,0:T(8,128)} %get-tuple-element.13.a1, f32[8,8,128]{2,1,0:T(8,128)} %get-tuple-element.14.a2, f32[3,1,2048]{2,1,0:T(1,128)} %get-tuple-element.15.a3), custom_call_target="tpu_custom_call" | custom-call | tf_op jit(solution)/shard_map/pallas_call | solution.py:781
